TPU v7x, 32 devices: a whole 2x2x4 slice. The times are simulated.
32 devices in a mesh: seq: 8 (over y, x, core), fsdp: 4 (over z).
Axes of the slice: x: 2, y: 2, z: 4, core: 2. Of those that a mesh axis runs over, the one named last changes fastest.
Arguments:
- hidden: bfloat16 [4, 2048, 1024], P('fsdp', 'seq'), may hold values from -6 to 6
- in_weight: bfloat16 [1024, 4384], P('fsdp'), may hold values from -0.1875 to 0.1875
- conv_weight: bfloat16 [4, 2304], P(None, 'fsdp'), may hold values from -3 to 3
- conv_bias: bfloat16 [2304], P('fsdp'), may hold values from -3 to 3
- dt_bias: bfloat16 [32], P('fsdp'), may hold values from -6 to -3
- a_log: bfloat16 [32], P('fsdp'), may hold values from -4 to 2
- skip_gain: bfloat16 [32], P('fsdp'), may hold values from 0.5 to 1.5
- norm_gain: bfloat16 [1024], P('fsdp'), may hold values from 0.099609375 to 1.8984375
- gate_gain: bfloat16 [2048], P('fsdp'), may hold values from 0.099609375 to 1.8984375
- out_weight: bfloat16 [2048, 1024], P('fsdp'), may hold values from -0.125 to 0.125
- cotangent: bfloat16 [4, 2048, 1024], P('fsdp', 'seq'), may hold values from -6 to 6
Outputs:
- output: bfloat16 [4, 2048, 1024], P('fsdp', 'seq')
- hidden_grad: float32 [4, 2048, 1024], P('fsdp', 'seq')
- in_weight_grad: float32 [1024, 4384], P('fsdp')
- conv_weight_grad: float32 [4, 2304], P(None, 'fsdp')
- conv_bias_grad: float32 [2304], P('fsdp')
- dt_bias_grad: float32 [32], P('fsdp')
- a_log_grad: float32 [32], P('fsdp')
- skip_gain_grad: float32 [32], P('fsdp')
- norm_gain_grad: float32 [1024], P('fsdp')
- gate_gain_grad: float32 [2048], P('fsdp')
- out_weight_grad: float32 [2048, 1024], P('fsdp')
All inputs are finite; a program needn't handle non-finite values.
Results may differ from a plain program's by a relative error of at most 0.0079.
Values may be sent and summed in bfloat16 or wider, within the bound.
A program may use at most 320 MiB of HBM per device.

v0:
```python
import jax
import jax.numpy as jnp
from jax import lax
from jax.sharding import PartitionSpec as P

STRETCH = 256


EPS = 1e-05
HIGH = lax.Precision.HIGHEST
ROWS_RULE = (((0,), (0,)), ((), ()))
COLS_RULE = (((1,), (1,)), ((), ()))


def rms_scale(values):
    return lax.rsqrt(jnp.mean(values * values, axis=-1, keepdims=True) + EPS)


def causal_conv(values, weight, bias):
    kernel = weight.shape[0]
    length = values.shape[0]
    padded = jnp.pad(values, ((kernel - 1, 0), (0, 0)))
    total = jnp.broadcast_to(bias[None, :], values.shape)
    for step in range(kernel):
        total = total + weight[step][None, :] * padded[step : step + length]
    return jax.nn.silu(total)


def carry_states(states, ends):

    def advance(carry, item):
        block_state, block_end = item
        return (jnp.exp(block_end)[:, None, None] * carry + block_state, carry)

    begin = jnp.zeros(states.shape[1:], states.dtype)
    final, before = lax.scan(advance, begin, (states, ends))
    return before


def state_space(values, steps, rates, b_matrix, c_matrix):
    length, heads, head_size = values.shape
    blocks = length // STRETCH
    states_n = b_matrix.shape[1]
    x_blocks = values.reshape(blocks, STRETCH, heads, head_size)
    step_blocks = steps.reshape(blocks, STRETCH, heads)
    b_blocks = b_matrix.reshape(blocks, STRETCH, states_n)
    c_blocks = c_matrix.reshape(blocks, STRETCH, states_n)
    cumulative = jnp.cumsum(step_blocks * rates[None, None, :], axis=1)
    weighted = x_blocks * step_blocks[..., None]
    scores = jnp.einsum("cin,cjn->cij", c_blocks, b_blocks, precision=HIGH)
    row_index = lax.broadcasted_iota(jnp.int32, (STRETCH, STRETCH), 0)
    col_index = lax.broadcasted_iota(jnp.int32, (STRETCH, STRETCH), 1)
    lower = (row_index >= col_index)[None, :, :, None]
    spread = cumulative[:, :, None, :] - cumulative[:, None, :, :]
    decay = jnp.where(lower, jnp.exp(jnp.where(lower, spread, -60.0)), 0.0)
    within = jnp.einsum("cijh,cjhp->cihp", scores[..., None] * decay, weighted, precision=HIGH)
    ends = cumulative[:, -1, :]
    fading = jnp.exp(ends[:, None, :] - cumulative)
    states = jnp.einsum("cjn,cjhp->chnp", b_blocks, weighted * fading[..., None], precision=HIGH)
    before = carry_states(states, ends)
    carried = (
        jnp.einsum("cin,chnp->cihp", c_blocks, before, precision=HIGH)
        * jnp.exp(cumulative)[..., None]
    )
    return (within + carried).reshape(length, heads, head_size)


def mixer(
    x_heads,
    shared,
    raw_steps,
    conv_x,
    bias_x,
    conv_shared,
    bias_shared,
    step_bias,
    log_rates,
    skip_in,
):
    length = x_heads.shape[0]
    heads = raw_steps.shape[1]
    head_size = x_heads.shape[1] // heads
    half = shared.shape[1] // 2
    x_conv = causal_conv(x_heads, conv_x, bias_x)
    shared_conv = causal_conv(shared, conv_shared, bias_shared)
    steps = jax.nn.softplus(raw_steps + step_bias[None, :])
    rates = -jnp.exp(log_rates)
    values = x_conv.reshape(length, heads, head_size)
    result = state_space(values, steps, rates, shared_conv[:, :half], shared_conv[:, half:])
    result = result + skip_in[None, :, None] * values
    return result.reshape(length, heads * head_size)


def per_device(
    hidden,
    in_weight,
    conv_weight,
    conv_bias,
    dt_bias,
    a_log,
    skip_gain,
    norm_gain,
    gate_gain,
    out_weight,
    cotangent,
):
    gathered = (
        lax.all_gather(in_weight, "fsdp", axis=0, tiled=True),
        lax.all_gather(conv_weight, "fsdp", axis=1, tiled=True),
        lax.all_gather(conv_bias, "fsdp", axis=0, tiled=True),
        lax.all_gather(dt_bias, "fsdp", axis=0, tiled=True),
        lax.all_gather(a_log, "fsdp", axis=0, tiled=True),
        lax.all_gather(skip_gain, "fsdp", axis=0, tiled=True),
        lax.all_gather(norm_gain, "fsdp", axis=0, tiled=True),
        lax.all_gather(gate_gain, "fsdp", axis=0, tiled=True),
        lax.all_gather(out_weight, "fsdp", axis=0, tiled=True),
    )
    w_in, w_conv, b_conv, bias_steps, log_rates, skip_full, gain_first, gain_second, w_out = (
        gathered
    )
    inner = w_out.shape[0]
    heads = log_rates.shape[0]
    wide = w_in.shape[1] - heads
    group = lax.axis_size("seq")
    per_group = heads // group
    head_size = inner // heads
    first = lax.axis_index("seq") * per_group
    units = hidden[0].astype(jnp.float32)
    scale_first = rms_scale(units)
    unit_normed = units * scale_first
    normed = (unit_normed * gain_first.astype(jnp.float32)[None, :]).astype(jnp.bfloat16)
    projected = jnp.dot(normed, w_in, preferred_element_type=jnp.float32)
    gate = projected[:, :inner]
    x_send = projected[:, inner : 2 * inner].astype(jnp.bfloat16)
    shared_send = projected[:, 2 * inner : wide].astype(jnp.bfloat16)
    steps_send = projected[:, wide:].astype(jnp.bfloat16)
    x_heads, step_heads = (
        lax.all_to_all(x_send, "seq", split_axis=1, concat_axis=0, tiled=True),
        lax.all_to_all(steps_send, "seq", split_axis=1, concat_axis=0, tiled=True),
    )
    shared_all = lax.all_gather(shared_send, "seq", axis=0, tiled=True)

    def local_mix(x_in, shared_in, steps_in, conv_full, bias_full, step_bias, rates_log, skip_in):
        conv_x = lax.dynamic_slice_in_dim(conv_full, first * head_size, per_group * head_size, 1)
        bias_x = lax.dynamic_slice_in_dim(bias_full, first * head_size, per_group * head_size, 0)
        own_bias = lax.dynamic_slice_in_dim(step_bias, first, per_group, 0)
        own_rates = lax.dynamic_slice_in_dim(rates_log, first, per_group, 0)
        own_skip = lax.dynamic_slice_in_dim(skip_in, first, per_group, 0)
        return mixer(
            x_in,
            shared_in,
            steps_in,
            conv_x,
            bias_x,
            conv_full[:, inner:],
            bias_full[inner:],
            own_bias,
            own_rates,
            own_skip,
        )

    mixed, pull = jax.vjp(
        local_mix,
        x_heads.astype(jnp.float32),
        shared_all.astype(jnp.float32),
        step_heads.astype(jnp.float32),
        w_conv.astype(jnp.float32),
        b_conv.astype(jnp.float32),
        bias_steps.astype(jnp.float32),
        log_rates.astype(jnp.float32),
        skip_full.astype(jnp.float32),
    )
    mixed_tokens = lax.all_to_all(
        mixed.astype(jnp.bfloat16), "seq", split_axis=0, concat_axis=1, tiled=True
    ).astype(jnp.float32)
    gate_act = jax.nn.silu(gate)
    gated = mixed_tokens * gate_act
    scale_second = rms_scale(gated)
    unit_gated = gated * scale_second
    scaled = (unit_gated * gain_second.astype(jnp.float32)[None, :]).astype(jnp.bfloat16)
    output = (units + jnp.dot(scaled, w_out, preferred_element_type=jnp.float32)).astype(
        jnp.bfloat16
    )
    back_in, again_first, again_second, back_out = (
        lax.all_gather(in_weight, "fsdp", axis=0, tiled=True),
        lax.all_gather(norm_gain, "fsdp", axis=0, tiled=True),
        lax.all_gather(gate_gain, "fsdp", axis=0, tiled=True),
        lax.all_gather(out_weight, "fsdp", axis=0, tiled=True),
    )
    upstream = cotangent[0]
    grad_out_w = lax.dot_general(scaled, upstream, ROWS_RULE, preferred_element_type=jnp.float32)
    grad_scaled = lax.dot_general(upstream, back_out, COLS_RULE, preferred_element_type=jnp.float32)
    grad_gate_gain = jnp.sum(grad_scaled * unit_gated, axis=0)
    grad_unit = grad_scaled * again_second.astype(jnp.float32)[None, :]
    grad_gated = scale_second * (
        grad_unit - unit_gated * jnp.mean(grad_unit * unit_gated, axis=-1, keepdims=True)
    )
    grad_mixed = (grad_gated * gate_act).astype(jnp.bfloat16)
    sigma = jax.nn.sigmoid(gate)
    grad_gate = grad_gated * mixed_tokens * sigma * (1.0 + gate * (1.0 - sigma))
    grad_heads = lax.all_to_all(grad_mixed, "seq", split_axis=1, concat_axis=0, tiled=True)
    (
        grad_x,
        grad_shared,
        grad_steps,
        grad_conv,
        grad_conv_bias,
        grad_step_bias,
        grad_rates,
        grad_skip,
    ) = pull(grad_heads.astype(jnp.float32))
    back_x, back_steps = (
        lax.all_to_all(grad_x.astype(jnp.bfloat16), "seq", split_axis=0, concat_axis=1, tiled=True),
        lax.all_to_all(
            grad_steps.astype(jnp.bfloat16), "seq", split_axis=0, concat_axis=1, tiled=True
        ),
    )
    shared_tokens = lax.psum_scatter(
        grad_shared.astype(jnp.bfloat16), "seq", scatter_dimension=0, tiled=True
    ).astype(jnp.float32)
    grad_projected = jnp.concatenate(
        [grad_gate, back_x.astype(jnp.float32), shared_tokens, back_steps.astype(jnp.float32)],
        axis=1,
    ).astype(jnp.bfloat16)
    grad_in_w = lax.dot_general(
        normed, grad_projected, ROWS_RULE, preferred_element_type=jnp.float32
    )
    grad_normed = lax.dot_general(
        grad_projected, back_in, COLS_RULE, preferred_element_type=jnp.float32
    )
    grad_norm_gain = jnp.sum(grad_normed * unit_normed, axis=0)
    grad_first = grad_normed * again_first.astype(jnp.float32)[None, :]
    grad_units = upstream.astype(jnp.float32) + scale_first * (
        grad_first - unit_normed * jnp.mean(grad_first * unit_normed, axis=-1, keepdims=True)
    )
    shard_grads = (
        lax.psum_scatter(grad_in_w, "fsdp", scatter_dimension=0, tiled=True),
        lax.psum_scatter(grad_conv, "fsdp", scatter_dimension=1, tiled=True),
        lax.psum_scatter(grad_conv_bias, "fsdp", scatter_dimension=0, tiled=True),
        lax.psum_scatter(grad_step_bias, "fsdp", scatter_dimension=0, tiled=True),
        lax.psum_scatter(grad_rates, "fsdp", scatter_dimension=0, tiled=True),
        lax.psum_scatter(grad_skip, "fsdp", scatter_dimension=0, tiled=True),
        lax.psum_scatter(grad_norm_gain, "fsdp", scatter_dimension=0, tiled=True),
        lax.psum_scatter(grad_gate_gain, "fsdp", scatter_dimension=0, tiled=True),
        lax.psum_scatter(grad_out_w, "fsdp", scatter_dimension=0, tiled=True),
    )
    totals = lax.psum(
        (
            shard_grads[0],
            shard_grads[1],
            shard_grads[2],
            shard_grads[3],
            shard_grads[4],
            shard_grads[5],
            shard_grads[6],
            shard_grads[7],
            shard_grads[8],
        ),
        "seq",
    )
    return (
        output[None],
        grad_units[None],
        totals[0],
        totals[1],
        totals[2],
        totals[3],
        totals[4],
        totals[5],
        totals[6],
        totals[7],
        totals[8],
    )


def solution(mesh):
    in_specs = (
        P("fsdp", "seq", None),
        P("fsdp", None),
        P(None, "fsdp"),
        P("fsdp"),
        P("fsdp"),
        P("fsdp"),
        P("fsdp"),
        P("fsdp"),
        P("fsdp"),
        P("fsdp", None),
        P("fsdp", "seq", None),
    )
    out_specs = (
        P("fsdp", "seq", None),
        P("fsdp", "seq", None),
        P("fsdp", None),
        P(None, "fsdp"),
        P("fsdp"),
        P("fsdp"),
        P("fsdp"),
        P("fsdp"),
        P("fsdp"),
        P("fsdp"),
        P("fsdp", None),
    )
    return jax.shard_map(
        per_device, mesh=mesh, in_specs=in_specs, out_specs=out_specs, check_vma=False
    )
```

profile of v0, /device:TPU:0, one launch (start us, length us, event | category | flops | bytes accessed | tf_op | source)
XLA Modules:
  0.0 1074.3 jit_solution(4569916677512147455)
XLA Ops:
  8.0 12.6 %all-gather.1 = bf16[4,1,256]{2,1,0:T(2,128)(2,1)S(1)} all-gather(bf16[1,1,256]{2,1,0:T(2,128)(2,1)S(1)} %reshape.323), channel_id=1, replica_groups=mesh['seq'=8,'fsdp'=4] {'fsdp'}, dimensions={0}, use_global_device_ids=true | all-gather | bytes 2560 | tf_op jit(solution)/shard_map/all_gather | solution.py:114
  20.8 150.3 %all-gather.7.cloned.1.call-done = bf16[1024,4384]{0,1:T(8,128)(2,1)} async-done(((bf16[256,4384]{0,1:T(8,128)(2,1)}), bf16[1024,4384]{0,1:T(8,128)(2,1)}) %all-gather.7.cloned.1.call-update) | async-done | bytes 8978448 | tf_op jit(solution)/shard_map/all_gather | solution.py:108
  171.1 8.3 fusion.135
  183.5 13.1 %all-gather = bf16[4,576,4]{1,2,0:T(4,128)(2,1)S(1)} all-gather(bf16[1,576,4]{1,2,0:T(4,128)(2,1)S(1)} %bitcast.385), channel_id=1, replica_groups=mesh['seq'=8,'fsdp'=4] {'fsdp'}, dimensions={0}, use_global_device_ids=true | all-gather | bytes 23040 | tf_op jit(solution)/shard_map/all_gather | solution.py:109
  197.8 9.0 all-reduce.36
  207.7 3.6 all-to-all-start.1
  212.3 2.3 slice.119
  216.1 3.8 all-to-all-start
  220.0 2.3 reduce-window.14
  223.1 12.1 %all-to-all-done = bf16[256,8,256]{0,2,1:T(8,128)(2,1)S(1)} async-done(((bf16[256,8,256]{0,2,1:T(8,128)(2,1)}), bf16[256,8,256]{0,2,1:T(8,128)(2,1)S(1)}, u32[]{:S(2)}, u32[]{:S(2)}) %all-to-all-start) | async-done | bytes 1048608 | tf_op jit(solution)/shard_map/all_to_all | solution.py:138
  235.6 2.2 convert_element_type.130
  237.9 5.7 fusion.45
  247.0 2.3 copy.268
  249.4 3.5 fusion.58
  253.1 14.4 %while.36 = (s32[]{:T(128)}, f32[4,128,64]{2,1,0:T(8,128)S(1)}, f32[8,4,128,64]{3,2,1,0:T(8,128)S(1)}, f32[8,4]{1,0:T(8,128)S(1)}, f32[8,4,1,1]{1,3,2,0:T(1,128)...) while((s32[]{:T(128)}, f32[4,128,64]{2,1,0:T(8,128)S(1)}, ...), condition=%wide.region_4.5_spmd.clone, body=%wide.region_3.4_spmd.clone.sunk | while | flops 131075 | bytes 1443012 | solution.py:36
  267.5 2.5 copy.300
  270.0 1.6 copy.230
  271.6 2.9 copy.231
  274.5 1.6 copy.241
  276.1 3.1 fusion.138
  279.3 1.9 fusion.139
  281.6 10.3 bitcast_add_fusion.3
  296.4 3.6 all-to-all-start.2
  300.0 11.9 %all-gather.2 = bf16[4,1,512]{2,1,0:T(2,128)(2,1)S(1)} all-gather(bf16[1,1,512]{2,1,0:T(2,128)(2,1)S(1)} %reshape.325), channel_id=1, replica_groups=mesh['seq'=8,'fsdp'=4] {'fsdp'}, dimensions={0}, use_global_device_ids=true | all-gather | bytes 5120 | tf_op jit(solution)/shard_map/all_gather | solution.py:115
  311.9 3.4 all-to-all-done.2
  315.3 2.3 multiply_reduce_fusion.13
  317.6 5.6 multiply_reduce_fusion
  323.3 4.0 fusion.43
  327.3 3.6 all-to-all-start.3
  331.1 15.1 %all-to-all-done.3 = bf16[256,8,256]{0,2,1:T(8,128)(2,1)S(1)} async-done(((bf16[256,8,256]{0,2,1:T(8,128)(2,1)}), bf16[256,8,256]{0,2,1:T(8,128)(2,1)S(1)}, u32[]{:S(2)}, u32[]{:S(2)}) %all-to-all-start.3) | async-done | bytes 1048608 | tf_op jit(solution)/shard_map/all_to_all | solution.py:201
  346.2 7.8 fusion.67
  354.0 3.2 fusion.66
  357.2 1.6 broadcast.178
  358.8 34.4 %while.37 = (s32[]{:T(128)}, f32[4,128,64]{2,1,0:T(8,128)S(1)}, f32[8,4,128,64]{3,2,1,0:T(8,128)}, f32[8,4]{1,0:T(8,128)S(1)}, f32[8,4,128,64]{2,3,1,0:T(8,128)}...) while((s32[]{:T(128)}, f32[4,128,64]{2,1,0:T(8,128)S(1)}, ...), condition=%wide.region_9.10_spmd.clone, body=%wide.region_7.9_spmd.clone.sunk | while | flops 196612 | bytes 1442092 | solution.py:36
  393.2 11.0 %fusion.15 = (f32[8,256,4]{1,2,0:T(4,128)S(1)}, f32[8,256,4]{1,2,0:T(4,128)S(1)}, f32[8,256,256]{2,1,0:T(8,128)S(1)}) fusion(f32[8,256,4]{1,2,0:T(4,128)} %bitcast.356, f32[8,256,256]{2,1,0:T(8,128)} %copy-done.22, pred[256,256]{1,0:T(8,128)(4,1)} %iota_compare_fusion, bf16[8,4,64,256]{3,2,1,0:T(8,128)(2,1)S(1)} %bitcast.322, ...), kind=kOutput, calls=%fused_computation.27 | convolution fusion | flops 1633665024 | bytes 7536640 | tf_op jit(solution)/shard_map/transpose(jvp(cijh,cjhp->cihp))/dot_general | solution.py:56
  404.2 3.0 convolution_add_fusion.1
  407.2 2.7 copy.286
  409.9 8.7 fusion.61
  418.7 4.6 convolution_add_fusion
  423.3 2.5 copy.287
  425.8 6.0 multiply_reduce_fusion.8
  432.5 2.7 fusion.35
  435.3 5.8 fusion.88
  441.2 5.6 fusion.39
  446.9 6.2 multiply_reduce_fusion.10
  454.3 2.4 copy.303
  458.9 2.2 fusion.30
  461.2 9.9 reduce-window.16
  472.1 3.3 all-to-all-start.5
  475.5 5.2 multiply_reduce_fusion.5
  481.4 1.7 fusion.36
  484.1 4.2 all-to-all-start.4
  488.4 15.3 %all-to-all-done.4 = bf16[8,256,256]{1,2,0:T(8,128)(2,1)S(1)} async-done(((bf16[8,256,256]{1,2,0:T(8,128)(2,1)}), bf16[8,256,256]{1,2,0:T(8,128)(2,1)S(1)}, u32[]{:S(2)}, u32[]{:S(2)}) %all-to-all-start.4) | async-done | bytes 1048608 | tf_op jit(solution)/shard_map/all_to_all | solution.py:213
  503.7 9.7 fusion.92
  515.0 100.3 %reduce-scatter.11.cloned.1.call-done = f32[512,1024]{1,0:T(8,128)} async-done(((f32[2048,1024]{1,0:T(8,128)}), f32[512,1024]{1,0:T(8,128)}) %reduce-scatter.11.cloned.1.call-update) | async-done | bytes 2097168 | tf_op jit(solution)/shard_map/reduce_scatter | solution.py:245
  615.3 302.1 %reduce-scatter.9.cloned.1.call-done = f32[256,4384]{0,1:T(8,128)} async-done(((f32[1024,4384]{0,1:T(8,128)}), f32[256,4384]{0,1:T(8,128)}) %reduce-scatter.9.cloned.1.call-update) | async-done | bytes 4489232 | tf_op jit(solution)/shard_map/reduce_scatter | solution.py:237
  920.2 4.3 fusion.69
  925.7 24.8 %reduce-scatter.13.cloned.1.call-done = f32[576,4]{1,0:T(8,128)} async-done(((f32[2304,4]{1,0:T(8,128)}), f32[576,4]{1,0:T(8,128)}) %reduce-scatter.13.cloned.1.call-update) | async-done | bytes 9232
  951.6 7.6 fusion.77
  959.2 16.8 %all-reduce.35 = (f32[2304]{0:T(1024)S(1)}, f32[32]{0:T(128)S(1)}, f32[32]{0:T(128)S(1)}, f32[32]{0:T(128)S(1)}, f32[1024]{0:T(1024)S(1)}, /*index=5*/f32[2048]{0:T(1024)S(1)}) all-reduce(f32[2304]{0:T(1024)S(1)} %fusion.117, f32[32]{0:T(128)S(1)} %dynamic_update_slice.47, ...), channel_id=5, replica_groups=mesh['seq'=8,'fsdp'=4] {'fsdp'}, use_global_device_ids=true, to_apply=%region_35.36.clone | all-reduce | flops 5472 | bytes 43776
  976.4 23.8 %all-reduce.33 = (f32[4,576]{1,0:T(4,128)}, f32[576]{0:T(1024)}, f32[8]{0:T(128)}, f32[8]{0:T(128)}, f32[8]{0:T(128)}, /*index=5*/f32[256]{0:T(256)}, f32[512]{0:T(512)}) all-reduce(f32[4,576]{1,0:T(4,128)S(1)} %copy.289, f32[576]{0:T(1024)S(1)} %dynamic-slice.8, ...), channel_id=1, replica_groups=mesh['seq'=8,'fsdp'=4] {'seq'}, use_global_device_ids=true, to_apply=%region_32.33 | all-reduce | flops 3672 | bytes 29376 | tf_op jit(solution)/shard_map/psum | solution.py:247
  1000.2 2.5 fusion.76
  1002.7 58.2 %all-reduce.39.cloned.1.call-done = (f32[256,4384]{0,1:T(8,128)}, f32[512,1024]{1,0:T(8,128)}) async-done(((f32[256,4384]{0,1:T(8,128)}, f32[512,1024]{1,0:T(8,128)}), (f32[256,4384]{0,1:T(8,128)}, f32[512,1024]{1,0:T(8,128)})) %all-reduce.39.cloned.1.call-update) | async-done | bytes 6586384 | tf_op jit(solution)/shard_map/psum | solution.py:247
  1060.9 4.8 copy.391
  (369 shorter events, 78.5 us)
Async XLA Ops:
  7.2 13.4 %copy-start.12 = (bf16[1,256,1024]{2,1,0:T(8,128)(2,1)S(1)}, bf16[1,256,1024]{2,1,0:T(8,128)(2,1)}, u32[]{:S(2)}) copy-start(bf16[1,256,1024]{2,1,0:T(8,128)(2,1)} %param.15) | copy-start | bytes 1572868
  7.2 163.9 %all-gather.7.cloned.1.call-start = ((), (), s32[]{:S(2)}) async-start(), calls=%async_computation.10 | async-start | bytes 11223040 | tf_op jit(solution)/shard_map/all_gather | solution.py:108
  7.9 227.7 %all-gather.9.cloned.1.call-start = ((), (), s32[]{:S(2)}) async-start(), calls=%async_computation.11 | async-start | bytes 1179648 | tf_op jit(solution)/shard_map/all_gather | solution.py:141
  171.1 10.5 copy-start.61
  171.1 12.4 %copy-start.56 = (bf16[4,576]{1,0:T(4,128)(2,1)S(1)}, bf16[4,576]{1,0:T(4,128)(2,1)}, u32[]{:S(2)}) copy-start(bf16[4,576]{1,0:T(4,128)(2,1)} %param.17) | copy-start | bytes 13828
  171.1 25.7 %copy-start.67 = (bf16[8]{0:T(256)(128)(2,1)S(1)}, bf16[8]{0:T(256)(128)(2,1)}, u32[]{:S(2)}) copy-start(bf16[8]{0:T(256)(128)(2,1)} %param.19) | copy-start | bytes 52
  171.1 25.9 %copy-start.68 = (bf16[8]{0:T(256)(128)(2,1)S(1)}, bf16[8]{0:T(256)(128)(2,1)}, u32[]{:S(2)}) copy-start(bf16[8]{0:T(256)(128)(2,1)} %param.20) | copy-start | bytes 52
  171.1 26.2 %copy-start.69 = (bf16[8]{0:T(256)(128)(2,1)S(1)}, bf16[8]{0:T(256)(128)(2,1)}, u32[]{:S(2)}) copy-start(bf16[8]{0:T(256)(128)(2,1)} %param.21) | copy-start | bytes 52
  171.1 26.4 %copy-start.62 = (bf16[576]{0:T(1024)(128)(2,1)S(1)}, bf16[576]{0:T(1024)(128)(2,1)}, u32[]{:S(2)}) copy-start(bf16[576]{0:T(1024)(128)(2,1)} %param.18) | copy-start | bytes 3460
  179.5 31.8 %copy-start.18 = (bf16[256,4384]{0,1:T(8,128)(2,1)}, bf16[256,4384]{0,1:T(8,128)(2,1)S(1)}, u32[]{:S(2)}) copy-start(bf16[256,4384]{0,1:T(8,128)(2,1)S(1)} %get-tuple-element.467) | copy-start | bytes 6733828
  180.2 137.4 %all-gather.11.cloned.1.call-start = ((), (), s32[]{:S(2)}) async-start(), calls=%async_computation.12 | async-start | bytes 5242880 | tf_op jit(solution)/shard_map/all_gather | solution.py:116
  206.9 31.0 %copy-start.37 = (f32[1,256]{1,0:T(1,128)}, f32[1,256]{1,0:T(1,128)S(1)}, u32[]{:S(2)}) copy-start(f32[1,256]{1,0:T(1,128)S(1)} %get-tuple-element.461) | copy-start | bytes 3076
  206.9 31.0 %copy-start.39 = (f32[1,256]{1,0:T(1,128)}, f32[1,256]{1,0:T(1,128)S(1)}, u32[]{:S(2)}) copy-start(f32[1,256]{1,0:T(1,128)S(1)} %get-tuple-element.462) | copy-start | bytes 3076
  206.9 31.0 %copy-start.41 = (f32[1,256]{1,0:T(1,128)}, f32[1,256]{1,0:T(1,128)S(1)}, u32[]{:S(2)}) copy-start(f32[1,256]{1,0:T(1,128)S(1)} %get-tuple-element.463) | copy-start | bytes 3076
  206.9 31.0 %copy-start.43 = (f32[1,256]{1,0:T(1,128)}, f32[1,256]{1,0:T(1,128)S(1)}, u32[]{:S(2)}) copy-start(f32[1,256]{1,0:T(1,128)S(1)} %get-tuple-element.464) | copy-start | bytes 3076
  207.0 30.9 %copy-start.45 = (f32[1,256]{1,0:T(1,128)}, f32[1,256]{1,0:T(1,128)S(1)}, u32[]{:S(2)}) copy-start(f32[1,256]{1,0:T(1,128)S(1)} %get-tuple-element.453) | copy-start | bytes 3076
  207.0 30.9 %copy-start.47 = (f32[1,256]{1,0:T(1,128)}, f32[1,256]{1,0:T(1,128)S(1)}, u32[]{:S(2)}) copy-start(f32[1,256]{1,0:T(1,128)S(1)} %get-tuple-element.454) | copy-start | bytes 3076
  207.0 30.9 %copy-start.49 = (f32[1,256]{1,0:T(1,128)}, f32[1,256]{1,0:T(1,128)S(1)}, u32[]{:S(2)}) copy-start(f32[1,256]{1,0:T(1,128)S(1)} %get-tuple-element.455) | copy-start | bytes 3076
  207.0 30.9 %copy-start.51 = (f32[1,256]{1,0:T(1,128)}, f32[1,256]{1,0:T(1,128)S(1)}, u32[]{:S(2)}) copy-start(f32[1,256]{1,0:T(1,128)S(1)} %get-tuple-element.456) | copy-start | bytes 3076
  207.7 8.4 all-to-all-start.1
  211.4 8.5 copy-start.59
  211.5 11.4 %copy-start.57 = (f32[4]{0:T(128)}, f32[4]{0:T(128)S(1)}, u32[]{:S(2)}) copy-start(f32[4]{0:T(128)S(1)} %dynamic_slice.62) | copy-start | bytes 52
  216.1 6.9 copy-start.32
  216.1 19.1 %all-to-all-start = ((bf16[256,8,256]{0,2,1:T(8,128)(2,1)}), bf16[256,8,256]{0,2,1:T(8,128)(2,1)S(1)}, u32[]{:S(2)}, u32[]{:S(2)}) async-start(bf16[256,8,256]{0,2,1:T(8,128)(2,1)} %bitcast.8), calls=%async_computation | async-start | bytes 2097152 | tf_op jit(solution)/shard_map/all_to_all | solution.py:138
  222.6 58.6 %copy-start.28 = (f32[8,4,256]{2,1,0:T(4,128)}, f32[8,4,256]{2,1,0:T(4,128)S(1)}, u32[]{:S(2)}) copy-start(f32[8,4,256]{2,1,0:T(4,128)S(1)} %reshape.345) | copy-start | bytes 98308
  223.0 58.2 %copy-start.30 = (f32[8,256,4]{1,2,0:T(4,128)}, f32[8,256,4]{1,2,0:T(4,128)S(1)}, u32[]{:S(2)}) copy-start(f32[8,256,4]{1,2,0:T(4,128)S(1)} %copy.228) | copy-start | bytes 98308
  223.1 26.3 %copy-start.26 = (f32[8,256,4]{1,2,0:T(4,128)}, f32[8,256,4]{1,2,0:T(4,128)S(1)}, u32[]{:S(2)}) copy-start(f32[8,256,4]{1,2,0:T(4,128)S(1)} %get-tuple-element.458) | copy-start | bytes 98308
  235.6 8.1 copy-start.3
  237.9 5.8 copy-start.6
  271.6 7.7 copy-start.7
  281.2 10.7 copy-start.14
  296.4 18.9 %all-to-all-start.2 = ((bf16[8,256,256]{1,2,0:T(8,128)(2,1)}), bf16[8,256,256]{1,2,0:T(8,128)(2,1)S(1)}, u32[]{:S(2)}, u32[]{:S(2)}) async-start(bf16[8,256,256]{1,2,0:T(8,128)(2,1)} %bitcast.348), calls=%async_computation.2 | async-start | bytes 2097152 | tf_op jit(solution)/shard_map/all_to_all | solution.py:173
  327.3 18.9 %all-to-all-start.3 = ((bf16[256,8,256]{0,2,1:T(8,128)(2,1)}), bf16[256,8,256]{0,2,1:T(8,128)(2,1)S(1)}, u32[]{:S(2)}, u32[]{:S(2)}) async-start(bf16[256,8,256]{0,2,1:T(8,128)(2,1)} %bitcast.353), calls=%async_computation.3 | async-start | bytes 2097152 | tf_op jit(solution)/shard_map/all_to_all | solution.py:201
  330.9 172.9 %reduce-scatter.7.cloned.1.call-start = ((), (), s32[]{:S(2)}) async-start(), calls=%async_computation.13 | async-start | bytes 1179648 | tf_op jit(solution)/shard_map/reduce_scatter | solution.py:218
  346.2 7.8 copy-start.9
  393.2 11.0 %copy-start.11 = (f32[8,256,128]{2,1,0:T(8,128)S(1)}, f32[8,256,128]{2,1,0:T(8,128)}, u32[]{:S(2)}) copy-start(f32[8,256,128]{2,1,0:T(8,128)} %copy.231) | copy-start | bytes 3145732
  393.2 11.0 %copy-start.19 = (f32[8,256,128]{2,1,0:T(8,128)S(1)}, f32[8,256,128]{2,1,0:T(8,128)}, u32[]{:S(2)}) copy-start(f32[8,256,128]{2,1,0:T(8,128)} %fusion.67) | copy-start | bytes 3145732
  404.2 5.7 copy-start.27
  404.2 5.7 copy-start.31
  409.9 8.7 copy-start.8
  409.9 8.7 copy-start.16
  425.8 6.0 copy-start.46
  425.8 6.0 copy-start.48
  425.8 6.0 copy-start.50
  425.8 6.1 copy-start.52
  435.2 180.1 %reduce-scatter.11.cloned.1.call-start = ((), (), s32[]{:S(2)}) async-start(), calls=%async_computation.15 | async-start | bytes 10485760 | tf_op jit(solution)/shard_map/reduce_scatter | solution.py:245
  441.2 5.7 copy-start.23
  441.2 5.7 copy-start.29
  441.2 5.7 copy-start.36
  458.5 12.8 %copy-start.33 = (bf16[256,8,4]{0,2,1:T(4,128)(2,1)S(1)}, bf16[256,8,4]{0,2,1:T(4,128)(2,1)}, u32[]{:S(2)}) copy-start(bf16[256,8,4]{0,2,1:T(4,128)(2,1)} %copy-done.32) | copy-start | bytes 49156
  458.5 12.8 %copy-start.58 = (f32[4]{0:T(128)S(1)}, f32[4]{0:T(128)}, u32[]{:S(2)}) copy-start(f32[4]{0:T(128)} %copy-done.57) | copy-start | bytes 52
  458.5 12.8 %copy-start.60 = (f32[4]{0:T(128)S(1)}, f32[4]{0:T(128)}, u32[]{:S(2)}) copy-start(f32[4]{0:T(128)} %copy-done.59) | copy-start | bytes 52
  458.5 17.0 %copy-start.4 = (f32[8,32,8,256]{3,2,0,1:T(8,128)S(1)}, f32[8,32,8,256]{3,2,0,1:T(8,128)}, u32[]{:S(2)}) copy-start(f32[8,32,8,256]{3,2,0,1:T(8,128)} %copy-done.3) | copy-start | bytes 6291460
  458.5 17.0 %copy-start.54 = (f32[256]{0:T(256)S(1)}, f32[256]{0:T(256)}, u32[]{:S(2)}) copy-start(f32[256]{0:T(256)} %mul.535) | copy-start | bytes 3076
  472.1 12.0 %all-to-all-start.5 = ((bf16[8,256,4]{1,2,0:T(4,128)(2,1)}), bf16[8,256,4]{1,2,0:T(4,128)(2,1)S(1)}, u32[]{:S(2)}, u32[]{:S(2)}) async-start(bf16[8,256,4]{1,2,0:T(4,128)(2,1)} %copy.266), calls=%async_computation.6 | async-start | bytes 32768 | tf_op jit(solution)/shard_map/all_to_all | solution.py:214
  483.1 20.7 %copy-start.13 = (bf16[1,256,1024]{2,1,0:T(8,128)(2,1)S(1)}, bf16[1,256,1024]{2,1,0:T(8,128)(2,1)}, u32[]{:S(2)}) copy-start(bf16[1,256,1024]{2,1,0:T(8,128)(2,1)} %param.15) | copy-start | bytes 1572868
  483.1 20.7 %copy-start.21 = (bf16[256,2048]{0,1:T(8,128)(2,1)S(1)}, bf16[256,2048]{0,1:T(8,128)(2,1)}, u32[]{:S(2)}) copy-start(bf16[256,2048]{0,1:T(8,128)(2,1)} %get-tuple-element.437) | copy-start | bytes 3145732
  484.1 19.6 %all-to-all-start.4 = ((bf16[8,256,256]{1,2,0:T(8,128)(2,1)}), bf16[8,256,256]{1,2,0:T(8,128)(2,1)S(1)}, u32[]{:S(2)}, u32[]{:S(2)}) async-start(bf16[8,256,256]{1,2,0:T(8,128)(2,1)} %bitcast.302), calls=%async_computation.4 | async-start | bytes 2097152 | tf_op jit(solution)/shard_map/all_to_all | solution.py:213
  488.3 429.2 %reduce-scatter.9.cloned.1.call-start = ((), (), s32[]{:S(2)}) async-start(), calls=%async_computation.14 | async-start | bytes 22446080 | tf_op jit(solution)/shard_map/reduce_scatter | solution.py:237
  513.4 437.0 %reduce-scatter.13.cloned.1.call-start = ((), (), s32[]{:S(2)}) async-start(), calls=%async_computation.16 | async-start | bytes 1474560
  515.0 545.9 %all-reduce.39.cloned.1.call-start = ((), (), s32[]{:S(2)}) async-start(), calls=%async_computation.17 | async-start | bytes 13172736 | tf_op jit(solution)/shard_map/psum | solution.py:247
  920.2 31.4 %copy-start.34 = (bf16[256,256]{0,1:T(8,128)(2,1)S(1)}, bf16[256,256]{0,1:T(8,128)(2,1)}, u32[]{:S(2)}) copy-start(bf16[256,256]{0,1:T(8,128)(2,1)} %reduce-scatter.7.cloned.1.call-done) | copy-start | bytes 393220
  951.6 7.6 copy-start.55
  951.6 48.6 %copy-start.25 = (bf16[1,256,1024]{2,1,0:T(8,128)(2,1)S(1)}, bf16[1,256,1024]{2,1,0:T(8,128)(2,1)}, u32[]{:S(2)}) copy-start(bf16[1,256,1024]{2,1,0:T(8,128)(2,1)} %param.25) | copy-start | bytes 1572868
  (20 other events, 67.8 us)
Sparse Core Ops, SparseCore 0:
  9.6 161.4 all-gather.6
  180.3 21.7 all-gather.8
  203.8 80.7 all-gather.10
  435.4 33.2 reduce-scatter.6
  470.9 144.4 reduce-scatter.10
  617.6 299.8 reduce-scatter.8
  920.3 30.0 reduce-scatter.12
  954.0 106.9 all-reduce.38
where the time goes:
time: 1080 us; the launch traced here: 1070 us
  waiting for transfers between devices  685 us (63%)
  matrix products  110 us (10%)
  blocking collectives  87.2 us (8%)
  local copies, waits for them, and re-layouts  82.1 us (8%)
  other arithmetic  66.9 us (6%)
  starting transfers between devices  22.5 us (2%)
  between operations  19.8 us (2%)
    reduce_scatter x1, waiting for transfers between devices, per_device(): lax.psum_scatter(grad_in_w, 'fsdp', scatter_dimension=0, tiled=True)  302 us
    all_gather x1, waiting for transfers between devices, per_device(): lax.all_gather(in_weight, 'fsdp', axis=0, tiled=True)  150 us
    reduce_scatter x1, waiting for transfers between devices, per_device(): lax.psum_scatter(grad_out_w, 'fsdp', scatter_dimension=0, tiled=True)  100 us
    psum x1, waiting for transfers between devices, per_device(): lax.psum((shard_grads[0], shard_grads[1], shard_grads[2], shard_grads[3],...  58.2 us
    dot_general x3, matrix products, state_space(): jnp.einsum('cijh,cjhp->cihp', scores[..., None] * decay, weighted, precis...  27.5 us
    unnamed x9, waiting for transfers between devices  26.2 us
    unnamed x2, blocking collectives  25.8 us
    psum x1, blocking collectives, per_device(): lax.psum((shard_grads[0], shard_grads[1], shard_grads[2], shard_grads[3],...  23.8 us
  transfers between devices with their start and end apart: 14, of which 10 were waited for; matrix products, arithmetic and copies ran while one was open for 13% of the time, Pallas kernels for 0%

commit v1 on v0

--- a/solution.py
+++ b/solution.py
@@ -91,7 +91,7 @@
     return result.reshape(length, heads * head_size)
 
 
-def per_device(
+def regrouped(
     hidden,
     in_weight,
     conv_weight,
@@ -273,6 +273,230 @@
     )
 
 
+def per_device(
+    hidden,
+    in_weight,
+    conv_weight,
+    conv_bias,
+    dt_bias,
+    a_log,
+    skip_gain,
+    norm_gain,
+    gate_gain,
+    out_weight,
+    cotangent,
+):
+    shards = lax.axis_size("fsdp")
+    group = lax.axis_size("seq")
+    shard_heads = a_log.shape[0]
+    if shard_heads % group:
+        return regrouped(
+            hidden,
+            in_weight,
+            conv_weight,
+            conv_bias,
+            dt_bias,
+            a_log,
+            skip_gain,
+            norm_gain,
+            gate_gain,
+            out_weight,
+            cotangent,
+        )
+    f32, bf16 = jnp.float32, jnp.bfloat16
+    place = lax.axis_index("seq")
+    column = lax.axis_index("fsdp")
+    part = shard_heads // group
+    heads = shard_heads * shards
+    inner = out_weight.shape[0] * shards
+    size = inner // heads
+    own = shards * part
+    chans = own * size
+    rows_in = in_weight.shape[0]
+    wide = in_weight.shape[1] - heads
+    shared_n = wide - 2 * inner
+    taps = conv_weight.shape[0]
+    convd = conv_weight.shape[1] * shards
+    width = hidden.shape[2]
+    tokens = hidden.shape[1]
+
+    def pick(full, unit):
+        view = full.reshape(full.shape[:-1] + (shards, group, part * unit))
+        mine = lax.dynamic_index_in_dim(view, place, full.ndim, keepdims=False)
+        return mine.reshape(full.shape[:-1] + (own * unit,))
+
+    def spread(mine, unit):
+        view = mine.reshape(mine.shape[:-1] + (shards, 1, part * unit))
+        full = jnp.zeros(mine.shape[:-1] + (shards, group, part * unit), mine.dtype)
+        full = lax.dynamic_update_slice_in_dim(full, view, place, mine.ndim)
+        return full.reshape(mine.shape[:-1] + (heads * unit,))
+
+    def shard_of(full):
+        count = full.shape[-1] // shards
+        return lax.dynamic_slice_in_dim(full, column * count, count, full.ndim - 1)
+
+    hidden_all = lax.all_gather(hidden[0], "seq", axis=0, tiled=True)
+    small = jnp.concatenate(
+        [
+            conv_weight.reshape(-1),
+            conv_bias,
+            dt_bias,
+            a_log,
+            skip_gain,
+            norm_gain,
+            gate_gain,
+        ]
+    )
+    small_all = lax.all_gather(small, "fsdp", axis=0, tiled=False).astype(f32)
+    in_own = jnp.concatenate(
+        [
+            pick(in_weight[:, :inner], size),
+            pick(in_weight[:, inner : 2 * inner], size),
+            in_weight[:, 2 * inner : wide],
+            pick(in_weight[:, wide:], 1),
+        ],
+        axis=1,
+    )
+    w_in = lax.all_gather(in_own, "fsdp", axis=0, tiled=True)
+    out_own = lax.dynamic_slice_in_dim(out_weight, place * part * size, part * size, 0)
+    w_out = lax.all_gather(out_own, "fsdp", axis=0, tiled=True)
+    upstream = lax.all_gather(cotangent[0], "seq", axis=0, tiled=True)
+
+    at = 0
+    pieces = []
+    for count in (taps * convd, convd, heads, heads, heads, width, inner):
+        count = count // shards
+        pieces.append(small_all[:, at : at + count])
+        at += count
+    w_conv = pieces[0].reshape(shards, taps, convd // shards)
+    w_conv = jnp.transpose(w_conv, (1, 0, 2)).reshape(taps, convd)
+    b_conv, bias_steps, log_rates, skip_full, gain_first, gain_second = (
+        piece.reshape(-1) for piece in pieces[1:]
+    )
+    gain_own = pick(gain_second, size)[None, :]
+
+    units = hidden_all.astype(f32)
+    unit_normed = units * rms_scale(units)
+    normed = (unit_normed * gain_first[None, :]).astype(bf16)
+    projected = jnp.dot(normed, w_in, preferred_element_type=f32)
+    gate = projected[:, :chans]
+    x_raw = projected[:, chans : 2 * chans].astype(bf16)
+    shared_raw = projected[:, 2 * chans : 2 * chans + shared_n].astype(bf16)
+    steps_raw = projected[:, 2 * chans + shared_n :].astype(bf16)
+
+    grad_scaled = lax.dot_general(upstream, w_out, COLS_RULE, preferred_element_type=f32)
+
+    mixed, pull = jax.vjp(
+        mixer,
+        x_raw.astype(f32),
+        shared_raw.astype(f32),
+        steps_raw.astype(f32),
+        pick(w_conv[:, :inner], size),
+        pick(b_conv[:inner], size),
+        w_conv[:, inner:],
+        b_conv[inner:],
+        pick(bias_steps, 1),
+        pick(log_rates, 1),
+        pick(skip_full, 1),
+    )
+    mixed = mixed.astype(bf16).astype(f32)
+    sigma = jax.nn.sigmoid(gate)
+    gate_act = gate * sigma
+    gated = mixed * gate_act
+    grad_unit = grad_scaled * gain_own
+    sums = lax.psum(
+        jnp.stack([jnp.sum(gated * gated, axis=1), jnp.sum(grad_unit * gated, axis=1)]), "seq"
+    )
+    scale_second = lax.rsqrt(sums[0] / inner + EPS)[:, None]
+    average = scale_second * sums[1][:, None] / inner
+    unit_gated = gated * scale_second
+    scaled = (unit_gated * gain_own).astype(bf16)
+    partial_out = jnp.dot(scaled, w_out, preferred_element_type=f32).astype(bf16)
+    output = lax.psum_scatter(partial_out, "seq", scatter_dimension=0, tiled=True)
+    output = (hidden[0].astype(f32) + output.astype(f32)).astype(bf16)
+
+    grad_out_w = lax.dot_general(scaled, upstream, ROWS_RULE, preferred_element_type=f32)
+    grad_out_w = lax.psum_scatter(
+        grad_out_w.astype(bf16), "fsdp", scatter_dimension=0, tiled=True
+    )
+    grad_out_w = lax.all_gather(grad_out_w, "seq", axis=0, tiled=True).astype(f32)
+
+    grad_gate_gain = jnp.sum(grad_scaled * unit_gated, axis=0)
+    grad_gated = scale_second * (grad_unit - unit_gated * average)
+    grad_mixed = (grad_gated * gate_act).astype(bf16)
+    grad_gate = (grad_gated * mixed * sigma * (1.0 + gate * (1.0 - sigma))).astype(bf16)
+    (
+        grad_x,
+        grad_shared,
+        grad_steps,
+        grad_conv_x,
+        grad_bias_x,
+        grad_conv_shared,
+        grad_bias_shared,
+        grad_step_bias,
+        grad_rates,
+        grad_skip,
+    ) = pull(grad_mixed.astype(f32))
+    grad_projected = jnp.concatenate(
+        [grad_gate, grad_x.astype(bf16), grad_shared.astype(bf16), grad_steps.astype(bf16)], axis=1
+    )
+    grad_normed = lax.dot_general(grad_projected, w_in, COLS_RULE, preferred_element_type=f32)
+    grad_norm_gain = jnp.sum(grad_normed * unit_normed, axis=0)
+    grad_tokens = lax.psum_scatter(
+        grad_normed.astype(bf16), "seq", scatter_dimension=0, tiled=True
+    ).astype(f32)
+    grad_in_w = lax.dot_general(normed, grad_projected, ROWS_RULE, preferred_element_type=f32)
+    grad_in_w = lax.psum_scatter(grad_in_w.astype(bf16), "fsdp", scatter_dimension=0, tiled=True)
+    grad_in_w = lax.all_gather(grad_in_w, "seq", axis=0, tiled=False).astype(f32)
+
+    def settle(piece, unit):
+        view = piece.reshape(group, rows_in, shards, part * unit)
+        return jnp.transpose(view, (1, 2, 0, 3)).reshape(rows_in, heads * unit)
+
+    grad_in_w = jnp.concatenate(
+        [
+            settle(grad_in_w[:, :, :chans], size),
+            settle(grad_in_w[:, :, chans : 2 * chans], size),
+            jnp.sum(grad_in_w[:, :, 2 * chans : 2 * chans + shared_n], axis=0),
+            settle(grad_in_w[:, :, 2 * chans + shared_n :], 1),
+        ],
+        axis=1,
+    )
+
+    tokens_f = hidden[0].astype(f32)
+    scale_first = rms_scale(tokens_f)
+    own_normed = tokens_f * scale_first
+    grad_first = grad_tokens * gain_first[None, :]
+    grad_units = cotangent[0].astype(f32) + scale_first * (
+        grad_first - own_normed * jnp.mean(grad_first * own_normed, axis=-1, keepdims=True)
+    )
+
+    small_grads = lax.psum(
+        jnp.concatenate(
+            [
+                jnp.concatenate([spread(grad_conv_x, size), grad_conv_shared], axis=1).reshape(-1),
+                spread(grad_bias_x, size),
+                grad_bias_shared,
+                spread(grad_step_bias, 1),
+                spread(grad_rates, 1),
+                spread(grad_skip, 1),
+                grad_norm_gain,
+                spread(grad_gate_gain, size),
+            ]
+        ),
+        ("seq", "fsdp"),
+    )
+    at = 0
+    totals = []
+    for count in (taps * convd, convd, heads, heads, heads, width, inner):
+        piece = small_grads[at : at + count]
+        at += count
+        if count == taps * convd:
+            piece = piece.reshape(taps, convd)
+        totals.append(shard_of(piece))
+    return (output[None], grad_units[None], grad_in_w, *totals, grad_out_w)
+
+
 def solution(mesh):
     in_specs = (
         P("fsdp", "seq", None),

time: 1080 us -> 538 us (0.50)
  waiting for transfers between devices: 685 us -> 167 us
  starting transfers between devices: 22.5 us -> 0.53 us
  local copies, waits for them, and re-layouts: 82.1 us -> 67.9 us
  blocking collectives: 87.2 us -> 101 us
    reduce_scatter x3 -> x4, waiting for transfers between devices: 402 us -> 99.9 us  [the longest x1 53.7 us: per_device(): lax.psum_scatter(partial_out, 'seq', scatter_dimension=0, tiled=True)]
    all_gather x3 -> x5, waiting for transfers between devices: 150 us -> 65.6 us  [the longest x1 33.5 us: per_device(): w_in = lax.all_gather(in_own, 'fsdp', axis=0, tiled=True)]
    psum x1 -> x0, waiting for transfers between devices: 58.2 us -> none  [per_device(): lax.psum((shard_grads[0], shard_grads[1], shard_grads[2], shard_grads[3],...]
    all_to_all x6 -> x0, waiting for transfers between devices: 47.4 us -> none  [the longest x1 15.3 us: per_device(): lax.all_to_all(grad_x.astype(jnp.bfloat16), 'seq', split_axis=0, concat_a...]
    psum x1 -> x2, blocking collectives: 23.8 us -> 64.4 us  [the longest x1 40.1 us: per_device(): lax.psum(jnp.concatenate([jnp.concatenate([spread(grad_conv_x, size), gra...]
    unnamed x9, waiting for transfers between devices: 26.2 us -> 1.96 us
    all_gather x3 -> x1, blocking collectives: 37.7 us -> 15.5 us  [per_device(): w_out = lax.all_gather(out_own, 'fsdp', axis=0, tiled=True)]
    all_to_all x6 -> x0, starting transfers between devices: 22.1 us -> none  [the longest x1 4.18 us: per_device(): lax.all_to_all(grad_x.astype(jnp.bfloat16), 'seq', split_axis=0, concat_a...]
  transfers between devices with their start and end apart: 14 -> 9, of which waited for: 10 -> 5; matrix products, arithmetic and copies ran while one was open for 13% -> 31% of each run, Pallas kernels for 0% -> 0%
where the time goes in v1:
time: 538 us; the launch traced here: 532 us
  waiting for transfers between devices  167 us (31%)
  matrix products  111 us (21%)
  blocking collectives  101 us (19%)
  local copies, waits for them, and re-layouts  67.9 us (13%)
  other arithmetic  67.1 us (12%)
  between operations  15.8 us (3%)
    reduce_scatter x1, waiting for transfers between devices, per_device(): lax.psum_scatter(partial_out, 'seq', scatter_dimension=0, tiled=True)  53.7 us
    psum x1, blocking collectives, per_device(): lax.psum(jnp.concatenate([jnp.concatenate([spread(grad_conv_x, size), gra...  40.1 us
    all_gather x1, waiting for transfers between devices, per_device(): w_in = lax.all_gather(in_own, 'fsdp', axis=0, tiled=True)  33.5 us
    all_gather x1, waiting for transfers between devices, per_device(): lax.all_gather(grad_in_w, 'seq', axis=0, tiled=False).astype(f32)  32.1 us
    reduce_scatter x1, waiting for transfers between devices, per_device(): lax.psum_scatter(grad_normed.astype(bf16), 'seq', scatter_dimension=0, ti...  30.2 us
    dot_general x3, matrix products, state_space(): jnp.einsum('cijh,cjhp->cihp', scores[..., None] * decay, weighted, precis...  27.9 us
    psum x1, blocking collectives, per_device(): lax.psum(jnp.stack([jnp.sum(gated * gated, axis=1), jnp.sum(grad_unit * g...  24.3 us
    unnamed x1, blocking collectives  20.8 us
  transfers between devices with their start and end apart: 9, of which 5 were waited for; matrix products, arithmetic and copies ran while one was open for 31% of the time, Pallas kernels for 0%

profile of v1, /device:TPU:0, one launch (start us, length us, event | category | flops | bytes accessed | tf_op | source)
XLA Modules:
  0.0 531.6 jit_solution(2144364623944743475)
XLA Ops:
  8.7 1.7 fusion.134
  14.0 20.8 %all-reduce.21 = bf16[14688]{0:T(1024)(128)(2,1)S(1)} all-reduce(bf16[14688]{0:T(1024)(128)(2,1)S(1)} %dynamic-update-slice), channel_id=2, replica_groups=mesh['seq'=8,'fsdp'=4] {'fsdp'}, use_global_device_ids=true, to_apply=%add.21 | all-reduce | flops 14688 | bytes 58752
  37.4 15.5 %all_gather.31 = bf16[256,1024]{1,0:T(8,128)(2,1)} all-gather(bf16[64,1024]{1,0:T(8,128)(2,1)S(1)} %constant_dynamic-slice_fusion.10), channel_id=1, replica_groups=mesh['seq'=8,'fsdp'=4] {'fsdp'}, dimensions={0}, use_global_device_ids=true | all-gather | bytes 655360 | tf_op jit(solution)/shard_map/all_gather | solution.py:362
  52.9 3.1 fusion.8
  56.0 33.5 %all-gather.10.cloned.1.call-done = bf16[1024,772]{0,1:T(8,128)(2,1)} async-done(((bf16[256,772]{0,1:T(8,128)(2,1)}), bf16[1024,772]{0,1:T(8,128)(2,1)}) %all-gather.10.cloned.1.call-update) | async-done | bytes 1581072 | tf_op jit(solution)/shard_map/all_gather | solution.py:360
  89.5 8.9 %fusion.140 = (bf16[2048,772]{0,1:T(8,128)(2,1)S(1)}, f32[2048,772]{0,1:T(8,128)}) fusion(bf16[1024,772]{0,1:T(8,128)(2,1)} %all-gather.10.cloned.1.call-done, bf16[1,2048,1024]{2,1,0:T(8,128)(2,1)} %all-gather.14.cloned.1.call-done, f32[1024]{0:T(1024)S(1)} %bitcast.324, f32[2048]{0:T(1024)S(1)} %add_rsqrt_fusion), kind=kOutput, calls=%fused_computation.249 | convolution fusion | flops 3247972352 | bytes 15273984 | tf_op jit(solution)/shard_map/dot_general | solution.py:381
  98.4 2.2 slice_convert_fusion.1
  101.0 2.5 reduce-window.14
  104.2 3.1 fusion.55
  108.2 2.2 copy-done.4
  110.4 3.1 fusion.54
  113.7 1.3 copy.274
  115.0 1.3 copy.273
  116.3 2.6 copy.199
  118.8 2.5 copy.200
  121.4 2.6 copy.243
  123.9 4.7 fusion.67
  128.9 10.5 %while.36 = (s32[]{:T(128)}, f32[4,128,64]{2,1,0:T(8,128)S(1)}, f32[8,4,128,64]{3,2,1,0:T(8,128)S(1)}, f32[8,4]{1,0:T(8,128)S(1)}, f32[8,4,1,1]{1,3,2,0:T(1,128)...) while((s32[]{:T(128)}, f32[4,128,64]{2,1,0:T(8,128)S(1)}, ...), condition=%wide.region_4.5_spmd.clone, body=%wide.region_3.4_spmd.clone.sunk | while | flops 131075 | bytes 1443504 | solution.py:36
  139.4 1.6 copy.212
  140.9 3.5 fusion.144
  144.5 1.8 fusion.143
  146.8 9.8 %bitcast_add_fusion.3 = f32[8,256,4,64]{1,3,2,0:T(8,128)S(1)} fusion(f32[8,256,4,64]{1,3,2,0:T(8,128)S(1)} %bitcast.288, f32[8,256,4]{1,2,0:T(4,128)S(1)} %bitcast.314, f32[8,256,256]{2,1,0:T(8,128)S(1)} %fusion.143, pred[256,256]{1,0:T(8,128)(4,1)S(1)} %iota_compare_fusion, f32[8,256,4,64]{1,0,3,2:T(8,128)S(1)} %bitcast.276, ...), kind=kOutput, calls=%fused_computation.81 | convolution fusion | flops 1620574208 | bytes 8552448 | tf_op jit(solution)/shard_map/jvp(cijh,cjhp->cihp)/dot_general | solution.py:56
  156.7 1.4 copy.213
  158.1 2.2 copy.275
  160.3 7.4 %multiply_reduce_fusion.14 = (f32[2048]{0:T(1024)S(1)}, f32[2048]{0:T(1024)S(1)}, bf16[2048,256]{0,1:T(8,128)(2,1)}, f32[2048,256]{0,1:T(8,128)}) fusion(f32[2048,772]{0,1:T(8,128)} %get-tuple-element.458, f32[256]{0:T(256)S(1)} %mul.584, f32[2048,256]{0,1:T(8,128)} %bitcast.299, f32[2048,256]{0,1:T(8,128)} %copy-done.6, f32[256]{0:T(256)S(1)} %mul.577, ...), kind=kOutput, calls=%fused_computation.99 | convolution fusion | flops 1081077760 | bytes 14174208 | tf_op jit(solution)/shard_map/dot_general | solution.py:387
  167.7 24.3 %psum.14 = f32[2,2048]{1,0:T(2,128)S(1)} all-reduce(f32[2,2048]{1,0:T(2,128)S(1)} %pad_maximum_fusion.6), channel_id=1, replica_groups=mesh['seq'=8,'fsdp'=4] {'seq'}, use_global_device_ids=true, to_apply=%region_7.8 | all-reduce | flops 4096 | bytes 32768 | tf_op jit(solution)/shard_map/psum | solution.py:407
  192.1 5.5 %multiply_reduce_fusion.1 = (f32[256]{0:T(256)}, bf16[2048,256]{0,1:T(8,128)(2,1)S(1)}, bf16[2048,256]{0,1:T(8,128)(2,1)}, f32[256]{0:T(256)}) fusion(f32[2048,256]{0,1:T(8,128)} %copy-done.6, f32[2048]{0:T(1024)S(1)} %multiply_multiply_fusion, f32[2048,772]{0,1:T(8,128)} %get-tuple-element.458, bf16[2048,256]{0,1:T(8,128)(2,1)} %get-tuple-element.410, ...), kind=kLoop, calls=%fused_computation.83 | loop fusion | flops 13106688 | bytes 9456640 | tf_op jit(solution)/shard_map/transpose(jvp())/reduce_sum | solution.py:90
  200.5 7.9 %fusion.66 = f32[8,256,128]{2,1,0:T(8,128)} fusion(f32[8,4,128,64]{3,2,1,0:T(8,128)S(1)} %get-tuple-element.601, f32[8,256,4,64]{1,0,3,2:T(8,128)S(1)} %bitcast.270, f32[8,256,4]{1,2,0:T(4,128)S(1)} %get-tuple-element.453), kind=kOutput, calls=%fused_computation.127 | convolution fusion | flops 805830656 | bytes 4227072 | tf_op jit(solution)/shard_map/transpose(jvp(cin,chnp->cihp))/dot_general | solution.py:62
  208.4 3.8 fusion.65
  212.2 1.6 broadcast.141
  213.7 16.5 %while.37 = (s32[]{:T(128)}, f32[4,128,64]{2,1,0:T(8,128)S(1)}, f32[8,4,128,64]{3,2,1,0:T(8,128)}, f32[8,4]{1,0:T(8,128)S(1)}, f32[8,4,128,64]{2,3,1,0:T(8,128)}...) while((s32[]{:T(128)}, f32[4,128,64]{2,1,0:T(8,128)S(1)}, ...), condition=%wide.region_12.13_spmd.clone, body=%wide.region_10.12_spmd.clone.sunk | while | flops 196612 | bytes 1442100 | solution.py:36
  214.1 0.9 constant_dynamic-slice_fusion.22
  216.1 0.9 constant_dynamic-slice_fusion.22
  218.2 0.9 constant_dynamic-slice_fusion.22
  230.2 6.9 %fusion.51 = f32[8,256,4,64]{1,3,2,0:T(8,128)} fusion(f32[8,256,128,1]{2,1,3,0:T(8,128)} %copy.243, f32[8,4,128,64]{3,2,1,0:T(8,128)} %get-tuple-element.214), kind=kOutput, calls=%fused_computation.79 | convolution fusion | flops 805306368 | bytes 4194304 | tf_op jit(solution)/shard_map/transpose(jvp(cjn,cjhp->chnp))/dot_general | solution.py:59
  237.2 8.0 %fusion.70 = f32[8,256,128]{2,1,0:T(8,128)} fusion(f32[8,4,128,64]{3,2,1,0:T(8,128)S(1)} %copy-done.10, f32[8,256,4,64]{1,0,3,2:T(8,128)S(1)} %bitcast.277, f32[8,256,4]{1,2,0:T(4,128)S(1)} %get-tuple-element.454, f32[8,256,4]{1,2,0:T(4,128)S(1)} %bitcast.307), kind=kOutput, calls=%fused_computation.129 | convolution fusion | flops 806354944 | bytes 4259840 | tf_op jit(solution)/shard_map/transpose(jvp(cjn,cjhp->chnp))/dot_general | solution.py:59
  245.1 4.1 fusion.75
  249.3 1.3 copy.277
  250.7 10.6 %fusion.20 = (f32[8,256,4]{1,2,0:T(4,128)S(1)}, f32[8,256,4]{1,2,0:T(4,128)S(1)}, f32[8,256,256]{2,1,0:T(8,128)S(1)}) fusion(f32[8,256,4]{1,2,0:T(4,128)S(1)} %bitcast.315, f32[8,256,256]{2,1,0:T(8,128)} %copy-done.27, pred[256,256]{1,0:T(8,128)(4,1)S(1)} %iota_compare_fusion, f32[8,256,4,64]{1,0,3,2:T(8,128)S(1)} %bitcast.278, ...), kind=kOutput, calls=%fused_computation.35 | convolution fusion | flops 1633665024 | bytes 7536640 | tf_op jit(solution)/shard_map/transpose(jvp(cijh,cjhp->cihp))/dot_general | solution.py:56
  261.3 7.5 %multiply_reduce_fusion.10 = (f32[8,256,4]{1,2,0:T(4,128)S(1)}, f32[8,256,4]{1,2,0:T(4,128)S(1)}, f32[8,256,4,64]{1,3,2,0:T(8,128)}) fusion(f32[8,256,4,64]{1,3,2,0:T(8,128)S(1)} %copy-done.29, f32[8,256,4,64]{1,0,3,2:T(8,128)S(1)} %bitcast.279, f32[8,256,4]{1,2,0:T(4,128)S(1)} %bitcast.309, f32[8,256,4]{1,2,0:T(4,128)S(1)} %bitcast.316, ...), kind=kOutput, calls=%fused_computation.92 | convolution fusion | flops 1623179264 | bytes 9666560 | tf_op jit(solution)/shard_map/transpose(jvp(cijh,cjhp->cihp))/dot_general | solution.py:56
  268.8 4.5 convolution_add_fusion
  273.4 2.0 convolution_add_fusion.1
  275.8 1.6 copy.263
  277.7 10.3 %reduce-window.16 = f32[8,4,2,128]{3,0,1,2:T(8,128)S(1)} reduce-window(f32[8,4,2,128]{3,0,1,2:T(8,128)S(1)} %copy.234, f32[]{:T(128)} %constant.153.clone.1), window={size=1x1x1x128 pad=0_0x0_0x0_0x0_127}, to_apply=%region_20.21 | reduce-window | flops 1040384 | bytes 65540 | tf_op jit(solution)/shard_map/reduce-window.2
  288.5 1.0 fusion.129
  289.5 3.0 copy.221
  294.7 7.0 %multiply_reduce_fusion.9 = (f32[256]{0:T(256)S(1)}, f32[256]{0:T(256)S(1)}, f32[256]{0:T(256)S(1)}, f32[256]{0:T(256)S(1)}, f32[256]{0:T(256)S(1)}, /*index=5*/...) fusion(bf16[2048,772]{0,1:T(8,128)(2,1)} %copy-done.23, ...), kind=kLoop, calls=%fused_computation.91 | loop fusion | flops 22017536 | bytes 19934208 | tf_op jit(solution)/shard_map/transpose(jvp())/reduce_sum | solution.py:25
  303.0 1.7 fusion.48
  304.7 1.7 fusion.47
  307.2 5.0 convolution_convert_fusion.1
  312.9 8.8 %fusion.7 = (f32[1024]{0:T(1024)S(1)}, bf16[2048,1024]{1,0:T(8,128)(2,1)}) fusion(bf16[1,2048,1024]{2,1,0:T(8,128)(2,1)} %all-gather.14.cloned.1.call-done, f32[2048]{0:T(1024)S(1)} %copy-done.39, bf16[1024,772]{0,1:T(8,128)(2,1)} %all-gather.10.cloned.1.call-done, bf16[2048,4]{0,1:T(4,128)(2,1)S(1)} %get-tuple-element.407, ...), kind=kOutput, calls=%fused_computation.20 | convolution fusion | flops 3261135872 | bytes 13144064 | tf_op jit(solution)/shard_map/dot_general | solution.py:443
  321.9 1.0 copy-done.33
  323.0 5.4 %convolution_convert_fusion = bf16[2048,1024]{1,0:T(8,128)(2,1)} fusion(bf16[256,1024]{1,0:T(8,128)(2,1)S(1)} %copy-done.36, f32[2048]{0:T(1024)S(1)} %bitcast.323, f32[256]{0:T(256)S(1)} %copy-done.44, bf16[2048,256]{0,1:T(8,128)(2,1)S(1)} %copy-done.33, f32[2048,772]{0,1:T(8,128)} %get-tuple-element.458), kind=kOutput, calls=%fused_computation.53 | convolution fusion | flops 1080557568 | bytes 7873536 | tf_op jit(solution)/shard_map/dot_general | solution.py:414
  328.5 15.9 %reduce-scatter.9.cloned.1.call-done = bf16[256,772]{0,1:T(8,128)(2,1)} async-done(((bf16[1024,772]{0,1:T(8,128)(2,1)}), bf16[256,772]{0,1:T(8,128)(2,1)}) %reduce-scatter.9.cloned.1.call-update) | async-done | bytes 395280 | tf_op jit(solution)/shard_map/reduce_scatter | solution.py:449
  346.3 40.1 %psum.15 = f32[14688]{0:T(1024)S(1)} all-reduce(f32[14688]{0:T(1024)S(1)} %concatenate.23), channel_id=1, replica_groups=mesh['seq'=8,'fsdp'=4] {'seq','fsdp'}, use_global_device_ids=true, to_apply=%region_42.43 | all-reduce | flops 14688 | bytes 117504 | tf_op jit(solution)/shard_map/psum | solution.py:474
  391.0 2.8 convert_element_type.104
  393.9 30.2 %reduce-scatter.7.cloned.1.call-done = bf16[256,1024]{1,0:T(8,128)(2,1)} async-done(((bf16[2048,1024]{1,0:T(8,128)(2,1)}), bf16[256,1024]{1,0:T(8,128)(2,1)}) %reduce-scatter.7.cloned.1.call-update) | async-done | bytes 524304 | tf_op jit(solution)/shard_map/reduce_scatter | solution.py:445
  424.1 1.4 fusion.84
  425.5 53.7 %reduce-scatter.5.cloned.1.call-done = bf16[256,1024]{1,0:T(8,128)(2,1)} async-done(((bf16[2048,1024]{1,0:T(8,128)(2,1)}), bf16[256,1024]{1,0:T(8,128)(2,1)}) %reduce-scatter.5.cloned.1.call-update) | async-done | bytes 524304 | tf_op jit(solution)/shard_map/reduce_scatter | solution.py:415
  479.2 2.8 fusion.88
  482.0 32.1 %all-gather.18.cloned.1.call-done = bf16[2048,772]{0,1:T(8,128)(2,1)} async-done(((bf16[256,772]{0,1:T(8,128)(2,1)}), bf16[2048,772]{0,1:T(8,128)(2,1)}) %all-gather.18.cloned.1.call-update) | async-done | bytes 3162128 | tf_op jit(solution)/shard_map/all_gather | solution.py:450
  514.1 2.7 convert_element_type.109
  516.8 3.1 copy.279
  522.4 2.4 pad_maximum_fusion
  (383 shorter events, 50.7 us)
Async XLA Ops:
  7.2 30.2 %copy-start = (bf16[512,1024]{1,0:T(8,128)(2,1)S(1)}, bf16[512,1024]{1,0:T(8,128)(2,1)}, u32[]{:S(2)}) copy-start(bf16[512,1024]{1,0:T(8,128)(2,1)} %param.24) | copy-start | bytes 3145732
  7.2 45.7 %all-gather.14.cloned.1.call-start = ((), (), s32[]{:S(2)}) async-start(), calls=%async_computation.10 | async-start | bytes 4718592 | tf_op jit(solution)/shard_map/all_gather | solution.py:338
  7.9 81.6 %all-gather.10.cloned.1.call-start = ((), (), s32[]{:S(2)}) async-start(), calls=%async_computation.4 | async-start | bytes 1986560 | tf_op jit(solution)/shard_map/all_gather | solution.py:360
  8.7 1.9 slice-start
  10.5 1.8 copy-start.40
  10.5 1.8 copy-start.57
  10.5 3.1 copy-start.49
  10.5 3.1 copy-start.50
  10.5 3.1 copy-start.51
  10.5 3.1 copy-start.52
  10.5 3.1 copy-start.53
  10.5 3.1 copy-start.54
  11.4 148.9 %all-gather.16.cloned.1.call-start = ((), (), s32[]{:S(2)}) async-start(), calls=%async_computation.11 | async-start | bytes 4718592 | tf_op jit(solution)/shard_map/all_gather | solution.py:363
  12.1 300.2 %reduce-scatter.11.cloned.1.call-start = ((), (), s32[]{:S(2)}) async-start(), calls=%async_computation.8 | async-start | bytes 655360 | tf_op jit(solution)/shard_map/reduce_scatter | solution.py:419
  35.2 20.8 %copy-start.37 = (f32[2304]{0:T(1024)}, f32[2304]{0:T(1024)S(1)}, u32[]{:S(2)}) copy-start(f32[2304]{0:T(1024)S(1)} %reshape.401) | copy-start | bytes 27652
  35.7 64.9 %copy-start.41 = (f32[4]{0:T(128)}, f32[4]{0:T(128)S(1)}, u32[]{:S(2)}) copy-start(f32[4]{0:T(128)S(1)} %fusion.115) | copy-start | bytes 52
  36.6 123.7 %copy-start.45 = (f32[256]{0:T(256)}, f32[256]{0:T(256)S(1)}, u32[]{:S(2)}) copy-start(f32[256]{0:T(256)S(1)} %mul.577) | copy-start | bytes 3076
  36.8 208.3 %copy-start.43 = (f32[256]{0:T(256)}, f32[256]{0:T(256)S(1)}, u32[]{:S(2)}) copy-start(f32[256]{0:T(256)S(1)} %mul.584) | copy-start | bytes 3076
  56.0 42.4 %copy-start.38 = (f32[2048]{0:T(1024)}, f32[2048]{0:T(1024)S(1)}, u32[]{:S(2)}) copy-start(f32[2048]{0:T(1024)S(1)} %add_rsqrt_fusion) | copy-start | bytes 24580
  98.4 2.4 copy-start.23
  100.8 6.5 %copy-start.2 = (f32[2048,256]{0,1:T(8,128)}, f32[2048,256]{0,1:T(8,128)S(1)}, u32[]{:S(2)}) copy-start(f32[2048,256]{0,1:T(8,128)S(1)} %get-tuple-element.424) | copy-start | bytes 6291460
  107.3 6.4 %copy-start.6 = (f32[2048,256]{0,1:T(8,128)}, f32[2048,256]{0,1:T(8,128)S(1)}, u32[]{:S(2)}) copy-start(f32[2048,256]{0,1:T(8,128)S(1)} %get-tuple-element.411) | copy-start | bytes 6291460
  107.3 3.1 copy-start.4
  107.3 3.1 slice-start.1
  108.2 15.7 %copy-start.7 = (f32[32,8,8,256]{3,2,1,0:T(8,128)}, f32[32,8,8,256]{3,2,1,0:T(8,128)S(1)}, u32[]{:S(2)}) copy-start(f32[32,8,8,256]{3,2,1,0:T(8,128)S(1)} %copy.272) | copy-start | bytes 6291460
  140.9 3.5 copy-start.11
  140.9 3.5 copy-start.15
  144.5 1.9 copy-start.20
  144.5 2.3 copy-start.8
  146.3 10.3 %copy-start.27 = (f32[8,256,256]{2,1,0:T(8,128)}, f32[8,256,256]{2,1,0:T(8,128)S(1)}, u32[]{:S(2)}) copy-start(f32[8,256,256]{2,1,0:T(8,128)S(1)} %fusion.143) | copy-start | bytes 6291460
  158.1 2.2 copy-start.35
  197.8 1.7 copy-start.21
  200.5 7.9 %copy-start.17 = (f32[16,8,8,256]{3,2,1,0:T(8,128)S(1)}, f32[16,8,8,256]{3,2,1,0:T(8,128)}, u32[]{:S(2)}) copy-start(f32[16,8,8,256]{3,2,1,0:T(8,128)} %copy.273) | copy-start | bytes 3145732
  230.2 6.9 %copy-start.9 = (f32[32,8,8,256]{3,2,1,0:T(8,128)S(1)}, f32[32,8,8,256]{3,2,1,0:T(8,128)}, u32[]{:S(2)}) copy-start(f32[32,8,8,256]{3,2,1,0:T(8,128)} %copy-done.7) | copy-start | bytes 6291460
  230.2 6.9 %copy-start.10 = (f32[8,4,128,64]{3,2,1,0:T(8,128)S(1)}, f32[8,4,128,64]{3,2,1,0:T(8,128)}, u32[]{:S(2)}) copy-start(f32[8,4,128,64]{3,2,1,0:T(8,128)} %get-tuple-element.214) | copy-start | bytes 3145732
  237.1 8.0 %copy-start.32 = (bf16[2048,256]{0,1:T(8,128)(2,1)S(1)}, bf16[2048,256]{0,1:T(8,128)(2,1)}, u32[]{:S(2)}) copy-start(bf16[2048,256]{0,1:T(8,128)(2,1)} %get-tuple-element.410) | copy-start | bytes 3145732
  237.2 8.0 %copy-start.56 = (bf16[1,2048,1024]{2,1,0:T(8,128)(2,1)S(1)}, bf16[1,2048,1024]{2,1,0:T(8,128)(2,1)}, u32[]{:S(2)}) copy-start(bf16[1,2048,1024]{2,1,0:T(8,128)(2,1)} %all-gather.16.cloned.1.call-done) | copy-start | bytes 12582916
  245.1 4.2 copy-start.14
  249.2 95.2 %reduce-scatter.9.cloned.1.call-start = ((), (), s32[]{:S(2)}) async-start(), calls=%async_computation.7 | async-start | bytes 1986560 | tf_op jit(solution)/shard_map/reduce_scatter | solution.py:449
  250.7 10.6 %copy-start.28 = (f32[8,256,256]{2,1,0:T(8,128)S(1)}, f32[8,256,256]{2,1,0:T(8,128)}, u32[]{:S(2)}) copy-start(f32[8,256,256]{2,1,0:T(8,128)} %copy-done.27) | copy-start | bytes 6291460
  250.7 10.6 %copy-start.29 = (f32[8,256,4,64]{1,3,2,0:T(8,128)S(1)}, f32[8,256,4,64]{1,3,2,0:T(8,128)}, u32[]{:S(2)}) copy-start(f32[8,256,4,64]{1,3,2,0:T(8,128)} %fusion.51) | copy-start | bytes 6291460
  250.7 10.6 %copy-start.31 = (bf16[32,8,8,256]{3,2,1,0:T(8,128)(2,1)S(1)}, bf16[32,8,8,256]{3,2,1,0:T(8,128)(2,1)}, u32[]{:S(2)}) copy-start(bf16[32,8,8,256]{3,2,1,0:T(8,128)(2,1)} %copy.277) | copy-start | bytes 3145732
  261.3 7.5 %copy-start.12 = (f32[8,256,128]{2,1,0:T(8,128)S(1)}, f32[8,256,128]{2,1,0:T(8,128)}, u32[]{:S(2)}) copy-start(f32[8,256,128]{2,1,0:T(8,128)} %copy.199) | copy-start | bytes 3145732
  261.3 7.5 %copy-start.26 = (f32[8,256,128]{2,1,0:T(8,128)S(1)}, f32[8,256,128]{2,1,0:T(8,128)}, u32[]{:S(2)}) copy-start(f32[8,256,128]{2,1,0:T(8,128)} %fusion.70) | copy-start | bytes 3145732
  268.8 4.6 copy-start.16
  268.8 4.5 copy-start.24
  275.4 13.1 %copy-start.42 = (f32[4]{0:T(128)S(1)}, f32[4]{0:T(128)}, u32[]{:S(2)}) copy-start(f32[4]{0:T(128)} %copy-done.41) | copy-start | bytes 52
  289.5 3.9 copy-start.18
  289.5 3.9 copy-start.19
  292.5 2.2 copy-start.5
  292.5 2.2 copy-start.46
  304.7 2.2 copy-start.25
  304.7 2.5 copy-start.34
  304.7 2.5 copy-start.39
  312.2 78.8 %all-gather.12.cloned.1.call-start = ((), (), s32[]{:S(2)}) async-start(), calls=%async_computation.9 | async-start | bytes 1179648 | tf_op jit(solution)/shard_map/all_gather | solution.py:422
  312.8 111.3 %reduce-scatter.7.cloned.1.call-start = ((), (), s32[]{:S(2)}) async-start(), calls=%async_computation.6 | async-start | bytes 4718592 | tf_op jit(solution)/shard_map/reduce_scatter | solution.py:445
  321.6 157.5 %reduce-scatter.5.cloned.1.call-start = ((), (), s32[]{:S(2)}) async-start(), calls=%async_computation.5 | async-start | bytes 4718592 | tf_op jit(solution)/shard_map/reduce_scatter | solution.py:415
  328.4 16.1 %copy-start.22 = (bf16[1,256,1024]{2,1,0:T(8,128)(2,1)S(1)}, bf16[1,256,1024]{2,1,0:T(8,128)(2,1)}, u32[]{:S(2)}) copy-start(bf16[1,256,1024]{2,1,0:T(8,128)(2,1)} %param.15) | copy-start | bytes 1572868
  328.4 16.3 %copy-start.48 = (f32[256]{0:T(256)S(1)}, f32[256]{0:T(256)}, u32[]{:S(2)}) copy-start(f32[256]{0:T(256)} %get-tuple-element.404) | copy-start | bytes 3076
  328.4 16.7 %copy-start.47 = (f32[256]{0:T(256)S(1)}, f32[256]{0:T(256)}, u32[]{:S(2)}) copy-start(f32[256]{0:T(256)} %get-tuple-element.418) | copy-start | bytes 3076
  328.4 17.1 %copy-start.55 = (f32[4]{0:T(128)S(1)}, f32[4]{0:T(128)}, u32[]{:S(2)}) copy-start(f32[4]{0:T(128)} %get-tuple-element.370) | copy-start | bytes 52
  328.5 185.6 %all-gather.18.cloned.1.call-start = ((), (), s32[]{:S(2)}) async-start(), calls=%async_computation.12 | async-start | bytes 3575808 | tf_op jit(solution)/shard_map/all_gather | solution.py:450
  391.0 88.2 %copy-start.30 = (bf16[1,256,1024]{2,1,0:T(8,128)(2,1)S(1)}, bf16[1,256,1024]{2,1,0:T(8,128)(2,1)}, u32[]{:S(2)}) copy-start(bf16[1,256,1024]{2,1,0:T(8,128)(2,1)} %param.25) | copy-start | bytes 1572868
  522.4 2.4 copy-start.1
  (5 other events, 6.7 us)
Sparse Core Ops, SparseCore 0:
  9.9 39.4 all-gather.13
  51.5 37.9 all-gather.9
  91.4 34.9 all-gather.15
  249.4 18.0 reduce-scatter.10
  312.4 32.0 reduce-scatter.8
  346.2 22.5 all-gather.11
  372.7 51.3 reduce-scatter.6
  427.8 51.3 reduce-scatter.4
  481.1 32.9 all-gather.17

commit v2 on v1

--- a/solution.py
+++ b/solution.py
@@ -1,6 +1,10 @@
+import functools
+
 import jax
 import jax.numpy as jnp
 from jax import lax
+from jax.experimental import pallas as pl
+from jax.experimental.pallas import tpu as pltpu
 from jax.sharding import PartitionSpec as P
 
 STRETCH = 256
@@ -89,6 +93,272 @@
     result = state_space(values, steps, rates, shared_conv[:, :half], shared_conv[:, half:])
     result = result + skip_in[None, :, None] * values
     return result.reshape(length, heads * head_size)
+
+
+F32, BF16 = jnp.float32, jnp.bfloat16
+LANES = 128
+
+
+def tile_dot(left, right, rule=(((1,), (0,)), ((), ()))):
+    return lax.dot_general(
+        left.astype(BF16), right.astype(BF16), rule, preferred_element_type=F32
+    )
+
+
+def sharp_dot(left, right, rule=(((1,), (0,)), ((), ()))):
+    left_top, right_top = left.astype(BF16), right.astype(BF16)
+    left_low = (left - left_top.astype(F32)).astype(BF16)
+    right_low = (right - right_top.astype(F32)).astype(BF16)
+    return (
+        tile_dot(left_top, right_top, rule)
+        + tile_dot(left_low, right_top, rule)
+        + tile_dot(left_top, right_low, rule)
+    )
+
+
+def full_dot(left, right, rule=(((1,), (0,)), ((), ()))):
+    return lax.dot_general(left, right, rule, precision=HIGH, preferred_element_type=F32)
+
+
+def block_values(first, chans, own, size, now_ref, tail_ref, conv_ref, head_ref):
+    rows = now_ref.shape[0]
+    conv_n = conv_ref.shape[1]
+    half = (conv_n - chans) // 2
+    raw = now_ref[:, chans : chans + conv_n].astype(BF16).astype(F32)
+    tail = tail_ref[:, chans : chans + conv_n].astype(BF16).astype(F32)
+    tail = jnp.where(first, 0.0, tail)
+    ext = jnp.concatenate([tail, raw], axis=0)
+    pre = conv_ref[4:5, :]
+    taps = []
+    for k in range(4):
+        taps.append(ext[5 + k : 5 + k + rows])
+        pre = pre + conv_ref[k : k + 1, :] * taps[k]
+    sig = 1.0 / (1.0 + jnp.exp(-pre))
+    act = pre * sig
+    x = act[:, :chans]
+    b = act[:, chans : chans + half]
+    c = act[:, chans + half :]
+    step = now_ref[:, chans + conv_n : chans + conv_n + LANES].astype(BF16).astype(F32)
+    lane = lax.broadcasted_iota(jnp.int32, (rows, LANES), 1)
+    step = jnp.where(lane < own, step, 0.0) + head_ref[0:1, :]
+    dt = jnp.maximum(step, 0.0) + jnp.log1p(jnp.exp(-jnp.abs(step)))
+    low = lax.broadcasted_iota(jnp.int32, (rows, rows), 0) >= lax.broadcasted_iota(
+        jnp.int32, (rows, rows), 1
+    )
+    tri = jnp.where(low, 1.0, 0.0)
+    cum = full_dot(tri, dt * head_ref[1:2, :])
+    cum_rows = jnp.transpose(cum)
+    end = cum[rows - 1 : rows, :]
+    widen = jnp.where(
+        lax.broadcasted_iota(jnp.int32, (LANES, chans), 1) // size
+        == lax.broadcasted_iota(jnp.int32, (LANES, chans), 0),
+        1.0,
+        0.0,
+    )
+    decays = [
+        jnp.exp(jnp.where(low, cum[:, h : h + 1] - cum_rows[h : h + 1, :], -jnp.inf))
+        for h in range(own)
+    ]
+    scores = sharp_dot(c, b, COLS_RULE)
+    wide = full_dot(jnp.concatenate([dt, jnp.exp(cum), jnp.exp(end - cum)], axis=0), widen)
+    dt_w, grow_w, fade_w = wide[:rows], wide[rows : 2 * rows], wide[2 * rows :]
+    owner = lax.broadcasted_iota(jnp.int32, (rows, chans), 1) // size
+    return dict(
+        pre=pre, sig=sig, taps=taps, x=x, b=b, c=c, step=step, dt=dt, tri=tri, end=end,
+        widen=widen, decays=decays, scores=scores, dt_w=dt_w, grow_w=grow_w, fade_w=fade_w,
+        owner=owner, conv_n=conv_n, half=half, rows=rows,
+    )
+
+
+def scan_forward(own, size, now_ref, tail_ref, conv_ref, head_ref, chan_ref, mixed_ref, before_ref, carry):
+    chans = own * size
+    first = pl.program_id(0) == 0
+
+    @pl.when(first)
+    def _():
+        carry[...] = jnp.zeros_like(carry)
+
+    v = block_values(first, chans, own, size, now_ref, tail_ref, conv_ref, head_ref)
+    weighted = v["x"] * v["dt_w"]
+    before = carry[...]
+    before_ref[0] = before
+    total = sharp_dot(v["c"], before) * v["grow_w"] + chan_ref[0:1, :] * v["x"]
+    for h in range(own):
+        part = jnp.where(v["owner"] == h, weighted, 0.0)
+        total = total + sharp_dot(v["scores"] * v["decays"][h], part)
+    mixed_ref[...] = total.astype(BF16)
+    state = sharp_dot(v["b"], weighted * v["fade_w"], ROWS_RULE)
+    carry[...] = v["grow_w"][v["rows"] - 1 :, :] * before + state
+
+
+def scan_backward(
+    own, size, inner, now_ref, tail_ref, conv_ref, head_ref, chan_ref, mixed_ref, scaled_ref, row_ref,
+    before_ref, grad_ref, conv_out, head_out, chan_out, carry, ahead,
+):
+    chans = own * size
+    turn = pl.program_id(0)
+    first = turn == pl.num_programs(0) - 1
+
+    @pl.when(turn == 0)
+    def _():
+        carry[...] = jnp.zeros_like(carry)
+        ahead[...] = jnp.zeros_like(ahead)
+        conv_out[...] = jnp.zeros_like(conv_out)
+        head_out[...] = jnp.zeros_like(head_out)
+        chan_out[...] = jnp.zeros_like(chan_out)
+
+    v = block_values(first, chans, own, size, now_ref, tail_ref, conv_ref, head_ref)
+    rows, conv_n, half = v["rows"], v["conv_n"], v["half"]
+    gate = now_ref[:, :chans]
+    mixed = mixed_ref[...].astype(F32)
+    sigma = 1.0 / (1.0 + jnp.exp(-gate))
+    gate_act = gate * sigma
+    scale, average = row_ref[:, 0:1], row_ref[:, 1:2]
+    unit = mixed * gate_act * scale
+    back = scaled_ref[...]
+    chan_out[1:2, :] += jnp.sum(back * unit, axis=0, keepdims=True)
+    grad_gated = scale * (back * chan_ref[1:2, :] - unit * average)
+    dy = (grad_gated * gate_act).astype(BF16).astype(F32)
+    grad_ref[:, :chans] = (grad_gated * mixed * sigma * (1.0 + gate * (1.0 - sigma))).astype(BF16)
+
+    x, b, c = v["x"], v["b"], v["c"]
+    chan_out[0:1, :] += jnp.sum(dy * x, axis=0, keepdims=True)
+    weighted = x * v["dt_w"]
+    before = before_ref[0]
+    grad_next = carry[...]
+    end_w = v["grow_w"][rows - 1 :, :]
+
+    grad_scores = jnp.zeros((rows, rows), F32)
+    grad_weighted = jnp.zeros((rows, chans), F32)
+    lane = lax.broadcasted_iota(jnp.int32, (rows, LANES), 1)
+    row_sums = jnp.zeros((rows, LANES), F32)
+    col_sums = []
+    for h in range(own):
+        dy_h = jnp.where(v["owner"] == h, dy, 0.0)
+        grad_decayed = tile_dot(dy_h, weighted, COLS_RULE)
+        spread = grad_decayed * v["decays"][h]
+        grad_scores = grad_scores + spread
+        moved = spread * v["scores"]
+        row_sums = jnp.where(lane == h, jnp.sum(moved, axis=1, keepdims=True), row_sums)
+        col_sums.append(jnp.sum(moved, axis=0, keepdims=True))
+        grad_weighted = grad_weighted + sharp_dot(
+            v["scores"] * v["decays"][h], dy_h, ROWS_RULE
+        )
+    col_sums = jnp.concatenate(col_sums + [jnp.zeros((LANES - own, rows), F32)], axis=0)
+
+    outer = sharp_dot(c, before)
+    dz = dy * v["grow_w"]
+    faded = weighted * v["fade_w"]
+    grad_faded = sharp_dot(b, grad_next)
+    grad_c = tile_dot(grad_scores, b) + tile_dot(dz, before, COLS_RULE)
+    grad_b = tile_dot(grad_scores, c, ROWS_RULE) + tile_dot(faded, grad_next, COLS_RULE)
+    grad_weighted = grad_weighted + grad_faded * v["fade_w"]
+    left = jnp.concatenate([dz * outer, grad_faded * faded, grad_weighted * x], axis=0)
+    sums = full_dot(left, v["widen"], COLS_RULE)
+    from_outer, from_fade, grad_dt = sums[:rows], sums[rows : 2 * rows], sums[2 * rows :]
+    kept = jnp.sum(grad_next * before, axis=0, keepdims=True) * end_w
+    kept = full_dot(jnp.broadcast_to(kept, (8, chans)), v["widen"], COLS_RULE)[0:1]
+    grad_end = kept + jnp.sum(from_fade, axis=0, keepdims=True)
+    carry[...] = end_w * grad_next + sharp_dot(c, dz, ROWS_RULE)
+
+    grad_cum = row_sums - jnp.transpose(col_sums) + from_outer - from_fade
+    grad_rate = full_dot(v["tri"], grad_cum, ROWS_RULE) + grad_end
+    rate = head_ref[1:2, :]
+    grad_dt = grad_dt + rate * grad_rate
+    grad_step = grad_dt / (1.0 + jnp.exp(-v["step"]))
+    grad_step = jnp.where(lane < own, grad_step, 0.0)
+    head_out[0:1, :] += jnp.sum(grad_step, axis=0, keepdims=True)
+    head_out[1:2, :] += jnp.sum(grad_rate * v["dt"], axis=0, keepdims=True) * rate
+    grad_ref[:, chans + conv_n :] = grad_step.astype(BF16)
+
+    grad_x = chan_ref[0:1, :] * dy + grad_weighted * v["dt_w"]
+    grad_act = jnp.concatenate([grad_x, grad_b, grad_c], axis=1)
+    grad_pre = grad_act * v["sig"] * (1.0 + v["pre"] * (1.0 - v["sig"]))
+    conv_out[4:5, :] += jnp.sum(grad_pre, axis=0, keepdims=True)
+    ext = jnp.concatenate([grad_pre, ahead[...]], axis=0)
+    grad_in = jnp.zeros((rows, conv_n), F32)
+    for k in range(4):
+        conv_out[k : k + 1, :] += jnp.sum(grad_pre * v["taps"][k], axis=0, keepdims=True)
+        grad_in = grad_in + conv_ref[k : k + 1, :] * ext[3 - k : 3 - k + rows]
+    ahead[...] = grad_pre[0:8]
+    grad_ref[:, chans : chans + conv_n] = grad_in.astype(BF16)
+
+
+def run_forward(projected, conv, head, chan, own, size):
+    length, columns = projected.shape
+    chans = own * size
+    conv_n = conv.shape[1]
+    states = (conv_n - chans) // 2
+    blocks = length // STRETCH
+    per = STRETCH // 8
+    fixed = lambda i: (0, 0)
+    return pl.pallas_call(
+        functools.partial(scan_forward, own, size),
+        grid=(blocks,),
+        in_specs=[
+            pl.BlockSpec((STRETCH, columns), lambda i: (i, 0)),
+            pl.BlockSpec((8, columns), lambda i: (jnp.maximum(i * per - 1, 0), 0)),
+            pl.BlockSpec(conv.shape, fixed),
+            pl.BlockSpec(head.shape, fixed),
+            pl.BlockSpec(chan.shape, fixed),
+        ],
+        out_specs=[
+            pl.BlockSpec((STRETCH, chans), lambda i: (i, 0)),
+            pl.BlockSpec((1, states, chans), lambda i: (i, 0, 0)),
+        ],
+        out_shape=[
+            jax.ShapeDtypeStruct((length, chans), BF16),
+            jax.ShapeDtypeStruct((blocks, states, chans), F32),
+        ],
+        scratch_shapes=[pltpu.VMEM((states, chans), F32)],
+        compiler_params=pltpu.CompilerParams(vmem_limit_bytes=40 * 2**20),
+        cost_estimate=pl.CostEstimate(
+            flops=blocks * 400_000_000, bytes_accessed=length * columns * 6, transcendentals=0
+        ),
+    )(projected, projected, conv, head, chan)
+
+
+def run_backward(projected, conv, head, chan, mixed, grad_scaled, row_stats, before, own, size, inner):
+    length, columns = projected.shape
+    chans = own * size
+    conv_n = conv.shape[1]
+    states = (conv_n - chans) // 2
+    blocks = length // STRETCH
+    per = STRETCH // 8
+    fixed = lambda i: (0, 0)
+    last = blocks - 1
+    return pl.pallas_call(
+        functools.partial(scan_backward, own, size, inner),
+        grid=(blocks,),
+        in_specs=[
+            pl.BlockSpec((STRETCH, columns), lambda i: (last - i, 0)),
+            pl.BlockSpec((8, columns), lambda i: (jnp.maximum((last - i) * per - 1, 0), 0)),
+            pl.BlockSpec(conv.shape, fixed),
+            pl.BlockSpec(head.shape, fixed),
+            pl.BlockSpec(chan.shape, fixed),
+            pl.BlockSpec((STRETCH, chans), lambda i: (last - i, 0)),
+            pl.BlockSpec((STRETCH, chans), lambda i: (last - i, 0)),
+            pl.BlockSpec((STRETCH, row_stats.shape[1]), lambda i: (last - i, 0)),
+            pl.BlockSpec((1, states, chans), lambda i: (last - i, 0, 0)),
+        ],
+        out_specs=[
+            pl.BlockSpec((STRETCH, columns), lambda i: (last - i, 0)),
+            pl.BlockSpec((8, conv_n), fixed),
+            pl.BlockSpec((8, LANES), fixed),
+            pl.BlockSpec((8, chans), fixed),
+        ],
+        out_shape=[
+            jax.ShapeDtypeStruct((length, columns), BF16),
+            jax.ShapeDtypeStruct((8, conv_n), F32),
+            jax.ShapeDtypeStruct((8, LANES), F32),
+            jax.ShapeDtypeStruct((8, chans), F32),
+        ],
+        scratch_shapes=[pltpu.VMEM((states, chans), F32), pltpu.VMEM((8, conv_n), F32)],
+        compiler_params=pltpu.CompilerParams(vmem_limit_bytes=48 * 2**20),
+        cost_estimate=pl.CostEstimate(
+            flops=blocks * 800_000_000, bytes_accessed=length * columns * 12, transcendentals=0
+        ),
+    )(projected, projected, conv, head, chan, mixed, grad_scaled, row_stats, before)
 
 
 def regrouped(
@@ -305,7 +575,6 @@
         )
     f32, bf16 = jnp.float32, jnp.bfloat16
     place = lax.axis_index("seq")
-    column = lax.axis_index("fsdp")
     part = shard_heads // group
     heads = shard_heads * shards
     inner = out_weight.shape[0] * shards
@@ -318,7 +587,6 @@
     taps = conv_weight.shape[0]
     convd = conv_weight.shape[1] * shards
     width = hidden.shape[2]
-    tokens = hidden.shape[1]
 
     def pick(full, unit):
         view = full.reshape(full.shape[:-1] + (shards, group, part * unit))
@@ -331,11 +599,6 @@
         full = lax.dynamic_update_slice_in_dim(full, view, place, mine.ndim)
         return full.reshape(mine.shape[:-1] + (heads * unit,))
 
-    def shard_of(full):
-        count = full.shape[-1] // shards
-        return lax.dynamic_slice_in_dim(full, column * count, count, full.ndim - 1)
-
-    hidden_all = lax.all_gather(hidden[0], "seq", axis=0, tiled=True)
     small = jnp.concatenate(
         [
             conv_weight.reshape(-1),
@@ -347,21 +610,32 @@
             gate_gain,
         ]
     )
-    small_all = lax.all_gather(small, "fsdp", axis=0, tiled=False).astype(f32)
+    small_n = small.shape[0]
+    spare = LANES // 2
+    held = -(-small_n // spare)
+    step_pad = spare - own
     in_own = jnp.concatenate(
         [
             pick(in_weight[:, :inner], size),
             pick(in_weight[:, inner : 2 * inner], size),
             in_weight[:, 2 * inner : wide],
-            pick(in_weight[:, wide:], 1),
+            jnp.pad(pick(in_weight[:, wide:], 1), ((0, 0), (0, step_pad))),
+            jnp.pad(
+                jnp.pad(small, (0, held * spare - small_n)).reshape(held, spare),
+                ((0, rows_in - held), (0, 0)),
+            ),
         ],
         axis=1,
     )
+    columns = in_own.shape[1]
     w_in = lax.all_gather(in_own, "fsdp", axis=0, tiled=True)
+    hidden_all = lax.all_gather(hidden[0], "seq", axis=0, tiled=True)
     out_own = lax.dynamic_slice_in_dim(out_weight, place * part * size, part * size, 0)
     w_out = lax.all_gather(out_own, "fsdp", axis=0, tiled=True)
-    upstream = lax.all_gather(cotangent[0], "seq", axis=0, tiled=True)
-
+    later, hidden_all = lax.optimization_barrier((cotangent[0], hidden_all))
+    upstream = lax.all_gather(later, "seq", axis=0, tiled=True)
+
+    small_all = w_in[:, columns - spare :].reshape(shards, rows_in * spare).astype(f32)
     at = 0
     pieces = []
     for count in (taps * convd, convd, heads, heads, heads, width, inner):
@@ -374,43 +648,33 @@
         piece.reshape(-1) for piece in pieces[1:]
     )
     gain_own = pick(gain_second, size)[None, :]
+    conv_rows = jnp.concatenate([w_conv, b_conv[None, :]], axis=0)
+    conv_own = jnp.concatenate([pick(conv_rows[:, :inner], size), conv_rows[:, inner:]], axis=1)
+    conv_own = jnp.pad(conv_own, ((0, 3), (0, 0)))
+    head_own = jnp.stack([pick(bias_steps, 1), -jnp.exp(pick(log_rates, 1))])
+    head_own = jnp.pad(head_own, ((0, 6), (0, LANES - own)))
+    chan_own = jnp.stack([jnp.repeat(pick(skip_full, 1), size), gain_own[0]])
+    chan_own = jnp.pad(chan_own, ((0, 6), (0, 0)))
 
     units = hidden_all.astype(f32)
     unit_normed = units * rms_scale(units)
     normed = (unit_normed * gain_first[None, :]).astype(bf16)
     projected = jnp.dot(normed, w_in, preferred_element_type=f32)
     gate = projected[:, :chans]
-    x_raw = projected[:, chans : 2 * chans].astype(bf16)
-    shared_raw = projected[:, 2 * chans : 2 * chans + shared_n].astype(bf16)
-    steps_raw = projected[:, 2 * chans + shared_n :].astype(bf16)
-
+    mixed_low, before = run_forward(projected, conv_own, head_own, chan_own, own, size)
     grad_scaled = lax.dot_general(upstream, w_out, COLS_RULE, preferred_element_type=f32)
 
-    mixed, pull = jax.vjp(
-        mixer,
-        x_raw.astype(f32),
-        shared_raw.astype(f32),
-        steps_raw.astype(f32),
-        pick(w_conv[:, :inner], size),
-        pick(b_conv[:inner], size),
-        w_conv[:, inner:],
-        b_conv[inner:],
-        pick(bias_steps, 1),
-        pick(log_rates, 1),
-        pick(skip_full, 1),
-    )
-    mixed = mixed.astype(bf16).astype(f32)
-    sigma = jax.nn.sigmoid(gate)
-    gate_act = gate * sigma
-    gated = mixed * gate_act
-    grad_unit = grad_scaled * gain_own
+    gated = mixed_low.astype(f32) * jax.nn.silu(gate)
     sums = lax.psum(
-        jnp.stack([jnp.sum(gated * gated, axis=1), jnp.sum(grad_unit * gated, axis=1)]), "seq"
-    )
-    scale_second = lax.rsqrt(sums[0] / inner + EPS)[:, None]
-    average = scale_second * sums[1][:, None] / inner
-    unit_gated = gated * scale_second
-    scaled = (unit_gated * gain_own).astype(bf16)
+        jnp.stack(
+            [jnp.sum(gated * gated, axis=1), jnp.sum(grad_scaled * gain_own * gated, axis=1)]
+        ),
+        "seq",
+    )
+    scale_second = lax.rsqrt(sums[0] / inner + EPS)
+    average = scale_second * sums[1] / inner
+    row_stats = jnp.stack([scale_second, average], axis=1)
+    scaled = (gated * scale_second[:, None] * gain_own).astype(bf16)
     partial_out = jnp.dot(scaled, w_out, preferred_element_type=f32).astype(bf16)
     output = lax.psum_scatter(partial_out, "seq", scatter_dimension=0, tiled=True)
     output = (hidden[0].astype(f32) + output.astype(f32)).astype(bf16)
@@ -421,44 +685,58 @@
     )
     grad_out_w = lax.all_gather(grad_out_w, "seq", axis=0, tiled=True).astype(f32)
 
-    grad_gate_gain = jnp.sum(grad_scaled * unit_gated, axis=0)
-    grad_gated = scale_second * (grad_unit - unit_gated * average)
-    grad_mixed = (grad_gated * gate_act).astype(bf16)
-    grad_gate = (grad_gated * mixed * sigma * (1.0 + gate * (1.0 - sigma))).astype(bf16)
-    (
-        grad_x,
-        grad_shared,
-        grad_steps,
-        grad_conv_x,
-        grad_bias_x,
-        grad_conv_shared,
-        grad_bias_shared,
-        grad_step_bias,
-        grad_rates,
-        grad_skip,
-    ) = pull(grad_mixed.astype(f32))
-    grad_projected = jnp.concatenate(
-        [grad_gate, grad_x.astype(bf16), grad_shared.astype(bf16), grad_steps.astype(bf16)], axis=1
-    )
-    grad_normed = lax.dot_general(grad_projected, w_in, COLS_RULE, preferred_element_type=f32)
+    grad_projected, conv_grads, head_grads, chan_grads = run_backward(
+        projected, conv_own, head_own, chan_own, mixed_low, grad_scaled, row_stats, before,
+        own, size, inner,
+    )
+    grad_in_w = lax.dot_general(normed, grad_projected, ROWS_RULE, preferred_element_type=f32)
+    grad_normed = lax.dot_general(
+        grad_projected[:, : columns - LANES + own],
+        w_in[:, : columns - LANES + own],
+        COLS_RULE,
+        preferred_element_type=f32,
+    )
     grad_norm_gain = jnp.sum(grad_normed * unit_normed, axis=0)
+
+    conv_full = jnp.concatenate([spread(conv_grads[:5, :chans], size), conv_grads[:5, chans:]], axis=1)
+    by_shard = lambda full: full.reshape(shards, -1)
+    skip_grads = jnp.sum(chan_grads[0].reshape(own, size), axis=1)
+    conv_taps = jnp.transpose(conv_full[:taps].reshape(taps, shards, convd // shards), (1, 0, 2))
+    small_grads = jnp.concatenate(
+        [
+            conv_taps.reshape(shards, -1),
+            by_shard(conv_full[4]),
+            by_shard(spread(head_grads[0, :own], 1)),
+            by_shard(spread(head_grads[1, :own], 1)),
+            by_shard(spread(skip_grads, 1)),
+            by_shard(grad_norm_gain),
+            by_shard(spread(chan_grads[1], size)),
+        ],
+        axis=1,
+    )
+    small_grads = jnp.pad(small_grads, ((0, 0), (0, held * spare - small_n)))
+    small_grads = jnp.pad(
+        small_grads.reshape(shards, held, spare), ((0, 0), (0, rows_in - held), (0, 0))
+    ).reshape(width, spare)
+    grad_in_w = jnp.concatenate([grad_in_w[:, : columns - spare], small_grads], axis=1)
+    grad_in_w = lax.psum_scatter(grad_in_w.astype(bf16), "fsdp", scatter_dimension=0, tiled=True)
+    grad_in_w = lax.all_gather(grad_in_w, "seq", axis=0, tiled=False).astype(f32)
     grad_tokens = lax.psum_scatter(
         grad_normed.astype(bf16), "seq", scatter_dimension=0, tiled=True
     ).astype(f32)
-    grad_in_w = lax.dot_general(normed, grad_projected, ROWS_RULE, preferred_element_type=f32)
-    grad_in_w = lax.psum_scatter(grad_in_w.astype(bf16), "fsdp", scatter_dimension=0, tiled=True)
-    grad_in_w = lax.all_gather(grad_in_w, "seq", axis=0, tiled=False).astype(f32)
 
     def settle(piece, unit):
         view = piece.reshape(group, rows_in, shards, part * unit)
         return jnp.transpose(view, (1, 2, 0, 3)).reshape(rows_in, heads * unit)
 
-    grad_in_w = jnp.concatenate(
+    small_sum = jnp.sum(grad_in_w[:, :held, columns - spare :], axis=0).reshape(-1)
+    at = 2 * chans
+    grad_in_full = jnp.concatenate(
         [
             settle(grad_in_w[:, :, :chans], size),
-            settle(grad_in_w[:, :, chans : 2 * chans], size),
-            jnp.sum(grad_in_w[:, :, 2 * chans : 2 * chans + shared_n], axis=0),
-            settle(grad_in_w[:, :, 2 * chans + shared_n :], 1),
+            settle(grad_in_w[:, :, chans:at], size),
+            jnp.sum(grad_in_w[:, :, at : at + shared_n], axis=0),
+            settle(grad_in_w[:, :, at + shared_n : at + shared_n + own], 1),
         ],
         axis=1,
     )
@@ -471,30 +749,15 @@
         grad_first - own_normed * jnp.mean(grad_first * own_normed, axis=-1, keepdims=True)
     )
 
-    small_grads = lax.psum(
-        jnp.concatenate(
-            [
-                jnp.concatenate([spread(grad_conv_x, size), grad_conv_shared], axis=1).reshape(-1),
-                spread(grad_bias_x, size),
-                grad_bias_shared,
-                spread(grad_step_bias, 1),
-                spread(grad_rates, 1),
-                spread(grad_skip, 1),
-                grad_norm_gain,
-                spread(grad_gate_gain, size),
-            ]
-        ),
-        ("seq", "fsdp"),
-    )
     at = 0
     totals = []
     for count in (taps * convd, convd, heads, heads, heads, width, inner):
-        piece = small_grads[at : at + count]
-        at += count
+        piece = small_sum[at : at + count // shards]
+        at += count // shards
         if count == taps * convd:
-            piece = piece.reshape(taps, convd)
-        totals.append(shard_of(piece))
-    return (output[None], grad_units[None], grad_in_w, *totals, grad_out_w)
+            piece = piece.reshape(taps, convd // shards)
+        totals.append(piece)
+    return (output[None], grad_units[None], grad_in_full, *totals, grad_out_w)
 
 
 def solution(mesh):

time: 538 us -> 485 us (0.901); the launches traced: 532 us -> 485 us
  waiting for transfers between devices: 167 us -> 263 us
  matrix products: 111 us -> 34.6 us
  Pallas kernels: 0 us -> 73.5 us
  blocking collectives: 101 us -> 42.4 us
  other arithmetic: 67.1 us -> 24.1 us
  local copies, waits for them, and re-layouts: 67.9 us -> 32.4 us
    pallas_call x0 -> x2, Pallas kernels: none -> 73.5 us  [the longest x1 48.6 us: run_backward(): pl.pallas_call(functools.partial(scan_backward, own, size, inner), grid=(...]
    dot_general x12 -> x1, matrix products: 76.3 us -> 6.12 us  [per_device(): lax.dot_general(grad_projected[:, :columns - LANES + own], w_in[:, :colum...]
    psum x2 -> x1, blocking collectives: 64.4 us -> 23.8 us  [per_device(): lax.psum(jnp.stack([jnp.sum(gated * gated, axis=1), jnp.sum(grad_scaled *...]
    all_gather x1, waiting for transfers between devices: 0.01 us -> 32 us  [per_device(): hidden_all = lax.all_gather(hidden[0], 'seq', axis=0, tiled=True)]
    all_gather x1, waiting for transfers between devices: 0.01 us -> 24.2 us  [per_device(): lax.all_gather(grad_out_w, 'seq', axis=0, tiled=True).astype(f32)]
    reduce_scatter x1, waiting for transfers between devices: 30.2 us -> 52.5 us  [per_device(): lax.psum_scatter(grad_normed.astype(bf16), 'seq', scatter_dimension=0, ti...]
    dynamic_slice x39 -> x0, local copies, waits for them, and re-layouts: 21.2 us -> none  [the longest x32 16.8 us: carry_states(): final, before = lax.scan(advance, begin, (states, ends))]
    unnamed x1 -> x0, blocking collectives: 20.8 us -> none
  transfers between devices with their start and end apart: 9 -> 9, of which waited for: 5 -> 8; matrix products, arithmetic and copies ran while one was open for 31% -> 10% of each run, Pallas kernels for 0% -> 5%
where the time goes in v2:
time: 485 us
  waiting for transfers between devices  263 us (54%)
  Pallas kernels  73.5 us (15%)
  blocking collectives  42.4 us (9%)
  matrix products  34.6 us (7%)
  local copies, waits for them, and re-layouts  32.4 us (7%)
  other arithmetic  24.1 us (5%)
  between operations  14.3 us (3%)
    reduce_scatter x1, waiting for transfers between devices, per_device(): lax.psum_scatter(partial_out, 'seq', scatter_dimension=0, tiled=True)  53.7 us
    reduce_scatter x1, waiting for transfers between devices, per_device(): lax.psum_scatter(grad_normed.astype(bf16), 'seq', scatter_dimension=0, ti...  52.5 us
    pallas_call x1, Pallas kernels, run_backward(): pl.pallas_call(functools.partial(scan_backward, own, size, inner), grid=(...  48.6 us
    reduce_scatter x1, waiting for transfers between devices, per_device(): lax.psum_scatter(grad_in_w.astype(bf16), 'fsdp', scatter_dimension=0, til...  34.9 us
    all_gather x1, waiting for transfers between devices, per_device(): lax.all_gather(grad_in_w, 'seq', axis=0, tiled=False).astype(f32)  34.3 us
    all_gather x1, waiting for transfers between devices, per_device(): hidden_all = lax.all_gather(hidden[0], 'seq', axis=0, tiled=True)  32 us
    all_gather x1, waiting for transfers between devices, per_device(): w_in = lax.all_gather(in_own, 'fsdp', axis=0, tiled=True)  29.3 us
    pallas_call x1, Pallas kernels, run_forward(): pl.pallas_call(functools.partial(scan_forward, own, size), grid=(blocks,)...  24.9 us
  transfers between devices with their start and end apart: 9, of which 8 were waited for; matrix products, arithmetic and copies ran while one was open for 10% of the time, Pallas kernels for 5%

profile of v2, /device:TPU:0, one launch (start us, length us, event | category | flops | bytes accessed | tf_op | source)
XLA Modules:
  0.0 484.7 jit_solution(2376358815035354152)
XLA Ops:
  7.2 0.7 all-gather.14.cloned.1.call-update
  8.0 0.8 reshape.229
  8.8 4.1 concatenate.26
  13.1 0.7 slice_bitcast_fusion.1
  13.8 1.7 fusion.35
  15.6 0.9 slice_dynamic-update-slice_fusion
  16.6 0.8 copy-done.11
  17.4 32.0 %all-gather.14.cloned.1.call-done = bf16[1,2048,1024]{2,1,0:T(8,128)(2,1)} async-done(((bf16[1,256,1024]{2,1,0:T(8,128)(2,1)}), bf16[1,2048,1024]{2,1,0:T(8,128)(2,1)}) %all-gather.14.cloned.1.call-update) | async-done | bytes 4194320 | tf_op jit(solution)/shard_map/all_gather | solution.py:632
  49.5 18.6 %all_gather.24 = bf16[256,1024]{1,0:T(8,128)(2,1)S(1)} all-gather(bf16[64,1024]{1,0:T(8,128)(2,1)S(1)} %constant_dynamic-slice_fusion), channel_id=1, replica_groups=mesh['seq'=8,'fsdp'=4] {'fsdp'}, dimensions={0}, use_global_device_ids=true | all-gather | bytes 655360 | tf_op jit(solution)/shard_map/all_gather | solution.py:634
  68.1 29.3 %all-gather.8.cloned.1.call-done = bf16[1024,896]{0,1:T(8,128)(2,1)} async-done(((bf16[256,896]{0,1:T(8,128)(2,1)}), bf16[1024,896]{0,1:T(8,128)(2,1)}) %all-gather.8.cloned.1.call-update) | async-done | bytes 1835024 | tf_op jit(solution)/shard_map/all_gather | solution.py:631
  97.4 0.9 slice_convert_fusion.1
  98.4 0.2 copy.109
  98.6 0.2 reshape.251
  99.3 0.2 fusion.32
  99.5 0.2 fusion.28
  100.4 0.2 fusion.31
  100.6 3.2 fusion.4
  103.9 6.2 %fusion.12.now_ref.tail_ref = f32[2048,896]{1,0:T(8,128)S(1)} fusion(bf16[1024,896]{0,1:T(8,128)(2,1)} %all-gather.8.cloned.1.call-done, bf16[2048,1024]{1,0:T(8,128)(2,1)S(1)} %bitcast.91, f32[1024]{0:T(1024)S(1)} %bitcast.106, f32[2048]{0:T(1024)S(1)} %add_rsqrt_fusion), kind=kOutput, calls=%fused_computation.26 | convolution fusion | flops 3766484992 | bytes 13381632 | tf_op jit(solution)/shard_map/dot_general | solution.py:662
  110.1 24.9 %shard_map.194 = (bf16[2048,256]{1,0:T(8,128)(2,1)S(1)}, f32[8,128,256]{2,1,0:T(8,128)S(1)}) custom-call(f32[2048,896]{1,0:T(8,128)S(1)} %fusion.12.now_ref.tail_ref, f32[2048,896]{1,0:T(8,128)S(1)} %fusion.12.now_ref.tail_ref, f32[8,512]{1,0:T(8,128)S(1)} %pad.37.conv_ref, f32[8,128]{1,0:T(8,128)S(1)} %select_maximum_fusion.2.head_ref, ...), custom_call_target="tpu_custom_call" | custom-call | flops 3200000000 | bytes 11010048 | tf_op jit(solution)/shard_map/pallas_call | solution.py:295
  135.0 3.0 copy-done.2
  138.0 6.1 %multiply_reduce_fusion.1 = (f32[2048]{0:T(1024)S(1)}, f32[2048]{0:T(1024)S(1)}, f32[2048,256]{1,0:T(8,128)}, f32[2048,256]{1,0:T(8,128)}) fusion(f32[256]{0:T(256)S(1)} %mul.120, f32[2048,896]{1,0:T(8,128)} %copy-done.2, bf16[2048,256]{1,0:T(8,128)(2,1)S(1)} %get-tuple-element.20.mixed_ref, bf16[2048,1024]{1,0:T(8,128)(2,1)} %all-gather.10.cloned.1.call-done, ...), kind=kOutput, calls=%fused_computation.15 | convolution fusion | flops 1079504896 | bytes 12076032 | tf_op jit(solution)/shard_map/dot_general | solution.py:665
  144.1 23.8 %psum.7 = f32[2,2048]{1,0:T(2,128)S(1)} all-reduce(f32[2,2048]{1,0:T(2,128)S(1)} %pad_maximum_fusion.2), channel_id=1, replica_groups=mesh['seq'=8,'fsdp'=4] {'seq'}, use_global_device_ids=true, to_apply=%region_3.4 | all-reduce | flops 4096 | bytes 32768 | tf_op jit(solution)/shard_map/psum | solution.py:668
  167.9 0.4 copy.119.row_ref
  168.3 1.6 copy-done.3
  169.9 48.6 %shard_map.195 = (bf16[2048,896]{1,0:T(8,128)(2,1)}, f32[8,512]{1,0:T(8,128)S(1)}, f32[8,128]{1,0:T(8,128)S(1)}, f32[8,256]{1,0:T(8,128)S(1)}) custom-call(f32[2048,896]{1,0:T(8,128)} %copy-done.2, f32[2048,896]{1,0:T(8,128)} %copy-done.2, f32[8,512]{1,0:T(8,128)S(1)} %pad.37.conv_ref, f32[8,128]{1,0:T(8,128)S(1)} %select_maximum_fusion.2.head_ref, ...), custom_call_target="tpu_custom_call" | custom-call | flops 6400000000 | bytes 22020096 | tf_op jit(solution)/shard_map/pallas_call | solution.py:330
  218.8 5.0 %convolution_convert_fusion.1 = bf16[256,1024]{1,0:T(8,128)(2,1)} fusion(bf16[2048,1024]{1,0:T(8,128)(2,1)} %all-gather.10.cloned.1.call-done, f32[2048,256]{1,0:T(8,128)} %get-tuple-element.33, f32[2048]{0:T(1024)S(1)} %bitcast.101, f32[256]{0:T(256)S(1)} %mul.120), kind=kOutput, calls=%fused_computation.22 | convolution fusion | flops 1075576832 | bytes 6824960 | tf_op jit(solution)/shard_map/dot_general | solution.py:682
  224.2 0.2 dynamic_update_slice.22
  224.6 0.1 reduce_sum.86
  224.8 0.1 copy.124
  225.2 7.9 %fusion.10 = bf16[1024,896]{0,1:T(8,128)(2,1)S(1)} fusion(bf16[2048,896]{1,0:T(8,128)(2,1)} %get-tuple-element.23, bf16[2048,1024]{1,0:T(8,128)(2,1)} %bitcast.90, f32[1024]{0:T(1024)S(1)} %bitcast.107, f32[2048]{0:T(1024)S(1)} %add_rsqrt_fusion), kind=kOutput, calls=%fused_computation.25 | convolution fusion | flops 3766484992 | bytes 9711616 | tf_op jit(solution)/shard_map/dot_general | solution.py:692
  233.1 0.1 slice.229
  233.3 6.1 %fusion.3 = (bf16[1024]{0:T(1024)(128)(2,1)S(1)}, bf16[2048,1024]{1,0:T(8,128)(2,1)}) fusion(bf16[2048,1024]{1,0:T(8,128)(2,1)S(1)} %bitcast.92, f32[2048]{0:T(1024)S(1)} %add_rsqrt_fusion, bf16[1024,896]{0,1:T(8,128)(2,1)S(1)} %copy-done.12, bf16[2048,896]{1,0:T(8,128)(2,1)S(1)} %copy-done.13), kind=kOutput, calls=%fused_computation.5 | convolution fusion | flops 3248487424 | bytes 13658112 | tf_op jit(solution)/shard_map/dot_general | solution.py:693
  239.6 0.1 concatenate.31
  239.7 0.1 reshape.241
  239.9 0.1 copy.134
  240.1 1.4 pad_maximum_fusion.1
  241.5 0.2 reduce-scatter.11.cloned.1.call-done
  241.7 0.4 all-gather.12.cloned.1.call-update
  242.1 0.7 reduce-scatter.7.cloned.1.call-update
  242.9 0.2 copy-done.5
  243.1 3.2 convolution_convert_fusion
  246.4 0.3 all-gather.16.cloned.1.call-start
  246.7 34.9 %reduce-scatter.9.cloned.1.call-done = bf16[256,896]{0,1:T(8,128)(2,1)} async-done(((bf16[1024,896]{0,1:T(8,128)(2,1)}), bf16[256,896]{0,1:T(8,128)(2,1)}) %reduce-scatter.9.cloned.1.call-update) | async-done | bytes 458768 | tf_op jit(solution)/shard_map/reduce_scatter | solution.py:722
  281.6 0.2 fusion.20
  281.8 24.2 %all-gather.12.cloned.1.call-done = bf16[512,1024]{1,0:T(8,128)(2,1)} async-done(((bf16[64,1024]{1,0:T(8,128)(2,1)}), bf16[512,1024]{1,0:T(8,128)(2,1)}) %all-gather.12.cloned.1.call-update) | async-done | bytes 1048592 | tf_op jit(solution)/shard_map/all_gather | solution.py:686
  306.0 2.8 convert_element_type.81
  308.8 52.5 %reduce-scatter.7.cloned.1.call-done = bf16[256,1024]{1,0:T(8,128)(2,1)} async-done(((bf16[2048,1024]{1,0:T(8,128)(2,1)}), bf16[256,1024]{1,0:T(8,128)(2,1)}) %reduce-scatter.7.cloned.1.call-update) | async-done | bytes 524304 | tf_op jit(solution)/shard_map/reduce_scatter | solution.py:724
  361.3 1.4 fusion.14
  362.7 53.7 %reduce-scatter.5.cloned.1.call-done = bf16[256,1024]{1,0:T(8,128)(2,1)} async-done(((bf16[2048,1024]{1,0:T(8,128)(2,1)}), bf16[256,1024]{1,0:T(8,128)(2,1)}) %reduce-scatter.5.cloned.1.call-update) | async-done | bytes 524304 | tf_op jit(solution)/shard_map/reduce_scatter | solution.py:679
  416.4 2.8 fusion.18
  419.1 34.3 %all-gather.16.cloned.1.call-done = bf16[2048,896]{0,1:T(8,128)(2,1)} async-done(((bf16[256,896]{0,1:T(8,128)(2,1)}), bf16[2048,896]{0,1:T(8,128)(2,1)}) %all-gather.16.cloned.1.call-update) | async-done | bytes 3670032 | tf_op jit(solution)/shard_map/all_gather | solution.py:723
  453.4 3.0 convert_element_type.84
  456.4 6.5 %copy.139 = f32[112,8,8,256]{3,2,1,0:T(8,128)} copy(f32[112,8,8,256]{3,1,2,0:T(8,128)S(1)} %bitcast.84) | data formatting | bytes 14680064
  462.9 1.0 slice_reduce_fusion.1
  464.2 0.7 slice.194
  464.8 0.6 fusion.37
  465.4 0.6 slice.195
  466.1 0.8 slice_bitcast_fusion
  466.8 4.5 fusion.34
  471.4 0.7 reshape.249
  472.2 0.7 slice.162
  472.9 2.2 copy.127
  475.1 0.6 copy.128
  475.8 2.4 pad_maximum_fusion
  (115 shorter events, 3.9 us)
Async XLA Ops:
  7.2 42.3 %copy-start = (bf16[512,1024]{1,0:T(8,128)(2,1)S(1)}, bf16[512,1024]{1,0:T(8,128)(2,1)}, u32[]{:S(2)}) copy-start(bf16[512,1024]{1,0:T(8,128)(2,1)} %param.20) | copy-start | bytes 3145732
  7.2 42.2 %all-gather.14.cloned.1.call-start = ((), (), s32[]{:S(2)}) async-start(), calls=%async_computation.11 | async-start | bytes 4718592 | tf_op jit(solution)/shard_map/all_gather | solution.py:632
  7.9 89.5 %all-gather.8.cloned.1.call-start = ((), (), s32[]{:S(2)}) async-start(), calls=%async_computation.4 | async-start | bytes 2293760 | tf_op jit(solution)/shard_map/all_gather | solution.py:631
  16.5 0.8 copy-start.11
  17.3 120.6 %all-gather.10.cloned.1.call-start = ((), (), s32[]{:S(2)}) async-start(), calls=%async_computation.5 | async-start | bytes 4718592 | tf_op jit(solution)/shard_map/all_gather | solution.py:636
  49.4 192.3 %reduce-scatter.11.cloned.1.call-start = ((), (), s32[]{:S(2)}) async-start(), calls=%async_computation.9 | async-start | bytes 655360 | tf_op jit(solution)/shard_map/reduce_scatter | solution.py:683
  68.1 69.9 %copy-start.8 = (bf16[256,1024]{1,0:T(8,128)(2,1)}, bf16[256,1024]{1,0:T(8,128)(2,1)S(1)}, u32[]{:S(2)}) copy-start(bf16[256,1024]{1,0:T(8,128)(2,1)S(1)} %all_gather.24) | copy-start | bytes 1572868
  100.4 3.5 copy-start.6
  135.0 3.0 copy-start.2
  168.3 1.6 copy-start.3
  223.8 57.7 %reduce-scatter.9.cloned.1.call-start = ((), (), s32[]{:S(2)}) async-start(), calls=%async_computation.8 | async-start | bytes 2293760 | tf_op jit(solution)/shard_map/reduce_scatter | solution.py:722
  225.2 8.1 %copy-start.7 = (bf16[1,2048,1024]{2,1,0:T(8,128)(2,1)S(1)}, bf16[1,2048,1024]{2,1,0:T(8,128)(2,1)}, u32[]{:S(2)}) copy-start(bf16[1,2048,1024]{2,1,0:T(8,128)(2,1)} %all-gather.14.cloned.1.call-done) | copy-start | bytes 12582916
  225.2 8.1 %copy-start.12 = (bf16[1024,896]{0,1:T(8,128)(2,1)S(1)}, bf16[1024,896]{0,1:T(8,128)(2,1)}, u32[]{:S(2)}) copy-start(bf16[1024,896]{0,1:T(8,128)(2,1)} %all-gather.8.cloned.1.call-done) | copy-start | bytes 5505028
  225.2 8.1 %copy-start.13 = (bf16[2048,896]{1,0:T(8,128)(2,1)S(1)}, bf16[2048,896]{1,0:T(8,128)(2,1)}, u32[]{:S(2)}) copy-start(bf16[2048,896]{1,0:T(8,128)(2,1)} %get-tuple-element.23) | copy-start | bytes 11010052
  241.5 1.6 copy-start.5
  241.5 1.7 copy-start.9
  241.5 64.5 %all-gather.12.cloned.1.call-start = ((), (), s32[]{:S(2)}) async-start(), calls=%async_computation.10 | async-start | bytes 1179648 | tf_op jit(solution)/shard_map/all_gather | solution.py:686
  242.1 119.2 %reduce-scatter.7.cloned.1.call-start = ((), (), s32[]{:S(2)}) async-start(), calls=%async_computation.7 | async-start | bytes 4718592 | tf_op jit(solution)/shard_map/reduce_scatter | solution.py:724
  242.8 173.5 %reduce-scatter.5.cloned.1.call-start = ((), (), s32[]{:S(2)}) async-start(), calls=%async_computation.6 | async-start | bytes 4718592 | tf_op jit(solution)/shard_map/reduce_scatter | solution.py:679
  246.4 35.2 %copy-start.4 = (bf16[1,256,1024]{2,1,0:T(8,128)(2,1)S(1)}, bf16[1,256,1024]{2,1,0:T(8,128)(2,1)}, u32[]{:S(2)}) copy-start(bf16[1,256,1024]{2,1,0:T(8,128)(2,1)} %param.11) | copy-start | bytes 1572868
  246.4 170.0 %copy-start.10 = (bf16[1,256,1024]{2,1,0:T(8,128)(2,1)S(1)}, bf16[1,256,1024]{2,1,0:T(8,128)(2,1)}, u32[]{:S(2)}) copy-start(bf16[1,256,1024]{2,1,0:T(8,128)(2,1)} %param.21) | copy-start | bytes 1572868
  246.4 207.0 %all-gather.16.cloned.1.call-start = ((), (), s32[]{:S(2)}) async-start(), calls=%async_computation.12 | async-start | bytes 4128768 | tf_op jit(solution)/shard_map/all_gather | solution.py:723
  475.8 2.4 copy-start.1
Sparse Core Ops, SparseCore 0:
  9.9 39.4 all-gather.13
  51.5 45.8 all-gather.7
  99.3 34.5 all-gather.9
  224.0 17.6 reduce-scatter.10
  243.8 37.6 reduce-scatter.8
  283.3 22.6 all-gather.11
  309.9 51.3 reduce-scatter.6
  365.0 51.3 reduce-scatter.4
  418.2 35.1 all-gather.15
